TPU v7x, 256 devices: a whole 4x4x8 slice. The times are simulated.
256 devices in a mesh: dom: 32 (over x, y, z_hi), edge: 8 (over z_lo, core).
Axes of the slice: x: 4, y: 4, z: 8 (z_hi: 2, z_lo: 4; z = z_hi * 4 + z_lo), core: 2. Of those that a mesh axis runs over, the one named last changes fastest.
Arguments:
- node_lat: bfloat16 [65536, 256], P(('dom', 'edge')), may hold values from -6 to 6
- edge_lat: bfloat16 [786432, 256], P(('dom', 'edge')), may hold values from -6 to 6
- senders: int32 [786432], P(('dom', 'edge')), may hold values from 0 to 6143
- receivers: int32 [786432], P(('dom', 'edge')), may hold values from 0 to 2047
- live_edges: int32 [32, 8], P('dom', 'edge'), may hold values from 768 to 3072, as said below
- send_rows: int32 [256, 4, 128], P(('dom', 'edge')), may hold values from 0 to 255, as said below
- edge_w1: bfloat16 [2, 768, 256], replicated, may hold values from -0.21875 to 0.21875
- edge_b1: float32 [2, 256], replicated, may hold values from -3 to 3
- edge_w2: bfloat16 [2, 256, 256], replicated, may hold values from -0.375 to 0.375
- edge_gain: float32 [2, 256], replicated, may hold values from 0.1 to 1.9
- node_w1: bfloat16 [2, 512, 256], replicated, may hold values from -0.25 to 0.25
- node_b1: float32 [2, 256], replicated, may hold values from -3 to 3
- node_w2: bfloat16 [2, 256, 256], replicated, may hold values from -0.375 to 0.375
- node_gain: float32 [2, 256], replicated, may hold values from 0.1 to 1.9
Outputs:
- node_out: bfloat16 [65536, 256], P(('dom', 'edge'))
- edge_out: bfloat16 [786432, 256], P(('dom', 'edge'))
Inputs may be any that keep to these rules, and one draw needn't show every extreme that they name: `send_rows`: for each device and face, 128 distinct rows of the device's own 256 nodes. `live_edges`: a multiple of 128 for every device; some device is full in every draw. `senders`: rows of the domain's node table. `receivers`: nodes of the edge's own domain.
All inputs are finite; a program needn't handle non-finite values.
Results may differ from a plain program's by a relative error of at most 0.014.
Values may be sent and summed in bfloat16 or wider, within the bound.
A program may use at most 64 MiB of HBM per device.

v0:
```python
import jax
import jax.numpy as jnp
from jax import lax
from jax.sharding import PartitionSpec as P

LAYERS = 2


eps_norm = 1e-05


def passed_along(value, axis, steps):
    count = lax.axis_size(axis)
    pairs = [(source, (source + steps) % count) for source in range(count)]
    return lax.ppermute(value, axis, pairs)


def layer_norm(values, norm_gain):
    center = values - jnp.mean(values, axis=-1, keepdims=True)
    spread = jnp.mean(center * center, axis=-1, keepdims=True)
    return center * lax.rsqrt(spread + eps_norm) * norm_gain


def edge_update(
    edge_rows, sender_rows, receiver_rows, weight_in, bias_in, weight_out, norm_gain, live_rows
):
    feature_width = edge_rows.shape[1]
    pre_act = jnp.dot(edge_rows, weight_in[:feature_width], preferred_element_type=jnp.float32)
    pre_act = pre_act + jnp.dot(
        sender_rows,
        weight_in[feature_width : 2 * feature_width],
        preferred_element_type=jnp.float32,
    )
    pre_act = pre_act + jnp.dot(
        receiver_rows, weight_in[2 * feature_width :], preferred_element_type=jnp.float32
    )
    hidden_rows = jax.nn.relu(pre_act + bias_in).astype(jnp.bfloat16)
    messages = layer_norm(
        jnp.dot(hidden_rows, weight_out, preferred_element_type=jnp.float32), norm_gain
    )
    messages = jnp.where(live_rows[:, None], messages, jnp.float32(0.0))
    return ((edge_rows.astype(jnp.float32) + messages).astype(jnp.bfloat16), messages)


def node_update(node_rows, aggregate, weight_in, bias_in, weight_out, norm_gain):
    feature_width = node_rows.shape[1]
    pre_act = jnp.dot(node_rows, weight_in[:feature_width], preferred_element_type=jnp.float32)
    pre_act = pre_act + jnp.dot(
        aggregate, weight_in[feature_width:], preferred_element_type=jnp.float32
    )
    hidden_rows = jax.nn.relu(pre_act + bias_in).astype(jnp.bfloat16)
    update = layer_norm(
        jnp.dot(hidden_rows, weight_out, preferred_element_type=jnp.float32), norm_gain
    )
    return (node_rows.astype(jnp.float32) + update).astype(jnp.bfloat16)


def shards(
    node_lat,
    edge_lat,
    senders,
    receivers,
    live_edges,
    send_rows,
    edge_w1,
    edge_b1,
    edge_w2,
    edge_gain,
    node_w1,
    node_b1,
    node_w2,
    node_gain,
):
    edge_rank = lax.axis_index("edge")
    rank_count = lax.axis_size("edge")
    domains = lax.axis_size("dom")
    stride = domains // 4
    offsets = (1, -1, stride, -stride)
    node_count = node_lat.shape[0]
    face_count = send_rows.shape[1]
    latent = node_lat.shape[1]
    live_rows = lax.broadcasted_iota(jnp.int32, (edge_lat.shape[0],), 0) < live_edges[0, 0]
    lists_all = None
    lists_all = lax.all_gather(send_rows, "edge", axis=0, tiled=True)
    lists_all = lists_all + (jnp.arange(rank_count, dtype=jnp.int32) * node_count)[:, None, None]
    owned_rows = node_lat
    edge_rows = edge_lat
    for layer_index in range(LAYERS):
        received = []
        domain_rows = lax.all_gather(owned_rows, "edge", axis=0, tiled=True)
        face_rows = jnp.take(domain_rows, lists_all, axis=0)
        for face_index in range(face_count):
            received.append(passed_along(face_rows[:, face_index], "dom", offsets[face_index]))
        halo_all = jnp.stack(received, axis=1).reshape(-1, latent)
        node_table = jnp.concatenate([domain_rows, halo_all], axis=0)
        sender_rows = jnp.take(node_table, senders, axis=0)
        receiver_rows = jnp.take(domain_rows, receivers, axis=0)
        edge_rows, messages = edge_update(
            edge_rows,
            sender_rows,
            receiver_rows,
            edge_w1[layer_index],
            edge_b1[layer_index],
            edge_w2[layer_index],
            edge_gain[layer_index],
            live_rows,
        )
        domain_sum = jax.ops.segment_sum(messages, receivers, num_segments=node_count * rank_count)
        summed = lax.dynamic_slice_in_dim(
            lax.psum(domain_sum.astype(jnp.bfloat16), "edge").astype(jnp.float32),
            edge_rank * node_count,
            node_count,
            0,
        )
        owned_rows = node_update(
            owned_rows,
            summed.astype(jnp.bfloat16),
            node_w1[layer_index],
            node_b1[layer_index],
            node_w2[layer_index],
            node_gain[layer_index],
        )
    return (owned_rows, edge_rows)


def solution(mesh):
    in_specs = (
        P(("dom", "edge"), None),
        P(("dom", "edge"), None),
        P(("dom", "edge")),
        P(("dom", "edge")),
        P("dom", "edge"),
        P(("dom", "edge"), None, None),
        P(),
        P(),
        P(),
        P(),
        P(),
        P(),
        P(),
        P(),
    )
    out_specs = (P(("dom", "edge"), None), P(("dom", "edge"), None))
    return jax.shard_map(shards, mesh=mesh, in_specs=in_specs, out_specs=out_specs, check_vma=False)
```

profile of v0, /device:TPU:1, one launch (start us, length us, event | category | flops | bytes accessed | tf_op | source)
XLA Modules:
  0.0 485.5 jit_solution(15923211818923466474)
XLA Ops:
  8.6 15.9 %all_gather.10 = s32[8,4,128]{2,1,0:T(4,128)S(1)} all-gather(s32[1,4,128]{2,1,0:T(4,128)} %param.25), channel_id=1, replica_groups=mesh['dom'=32,'edge'=8] {'edge'}, dimensions={0}, use_global_device_ids=true | all-gather | bytes 18432 | tf_op jit(solution)/shard_map/all_gather | solution.py:84
  28.8 19.3 %all-gather.3.cloned.1.call-done = bf16[2048,256]{1,0:T(8,128)(2,1)} async-done(((bf16[256,256]{1,0:T(8,128)(2,1)}), bf16[2048,256]{1,0:T(8,128)(2,1)}) %all-gather.3.cloned.1.call-update) | async-done | bytes 1048592 | tf_op jit(solution)/shard_map/all_gather | solution.py:90
  48.2 14.3 %gather_fusion = bf16[4096,256]{1,0:T(8,128)(2,1)S(1)} fusion(bf16[2048,256]{1,0:T(8,128)(2,1)} %all-gather.3.cloned.1.call-done, s32[4096]{0:T(1024)S(1)} %broadcast_clamp_fusion), kind=kCustom, calls=%fused_computation.clone | custom fusion | bytes 4210688 | tf_op jit(solution)/shard_map/jit(_take)/gather | solution.py:91
  67.1 4.8 collective-permute-start
  71.9 4.8 collective-permute-start.1
  77.3 3.2 fusion.76
  80.5 13.0 %gather_fusion.2 = bf16[3072,256]{1,0:T(8,128)(2,1)} fusion(bf16[2048,256]{1,0:T(8,128)(2,1)S(1)} %copy-done, s32[3072]{0:T(1024)S(1)} %fusion.103), kind=kCustom, calls=%fused_computation.2.clone | custom fusion | bytes 3158016 | tf_op jit(solution)/shard_map/jit(_take)/gather | solution.py:97
  93.5 18.0 %collective-permute-done = bf16[8,128,256]{2,1,0:T(8,128)(2,1)} collective-permute-done((bf16[8,128,256]{2,1,0:T(8,128)(2,1)S(1)}, bf16[8,128,256]{2,1,0:T(8,128)(2,1)}, u32[]{:S(2)}, u32[]{:S(2)}) %collective-permute-start) | collective-permute-done | bytes 524320 | tf_op jit(solution)/shard_map/ppermute | solution.py:15
  111.5 6.8 %collective-permute-done.1 = bf16[8,128,256]{2,1,0:T(8,128)(2,1)} collective-permute-done((bf16[8,128,256]{2,1,0:T(8,128)(2,1)S(1)}, bf16[8,128,256]{2,1,0:T(8,128)(2,1)}, u32[]{:S(2)}, u32[]{:S(2)}) %collective-permute-start.1) | collective-permute-done | bytes 524320 | tf_op jit(solution)/shard_map/ppermute | solution.py:15
  121.7 14.7 %gather_fusion.1 = bf16[3072,256]{1,0:T(8,128)(2,1)} fusion(bf16[6144,256]{1,0:T(8,128)(2,1)} %pad_maximum_fusion, s32[3072]{0:T(1024)S(1)} %fusion.102), kind=kCustom, calls=%fused_computation.1.clone | custom fusion | bytes 3158016 | tf_op jit(solution)/shard_map/jit(_take)/gather | solution.py:96
  136.4 3.7 convolution_add_fusion.3
  140.1 5.3 %fusion.122 = (f32[3072]{0:T(1024)S(1)}, f32[3072,256]{0,1:T(8,128)}) fusion(bf16[2,256,256]{2,1,0:T(8,128)(2,1)S(1)} %copy-done.10, f32[3072,256]{1,0:T(8,128)} %convolution_add_fusion.3, bf16[3072,256]{1,0:T(8,128)(2,1)} %gather_fusion.2, f32[256]{0:T(256)S(1)} %bitcast.134, pred[3072]{0:T(1024)(128)(4,1)S(1)} %compare_and_fusion.1, ...), kind=kOutput, calls=%fused_computation.157 | convolution fusion | flops 810021888 | bytes 8142848 | tf_op jit(solution)/shard_map/dot_general | solution.py:39
  149.5 19.3 %scatter_custom_fusion = f32[2048,256]{1,0:T(8,128)} fusion(s32[3072]{0:T(1024)} %param.23, f32[3072,256]{1,0:T(8,128)S(1)} %copy.53, f32[256]{0:T(256)S(1)} %bitcast.129, f32[3072]{0:T(1024)S(1)} %add_rsqrt_fusion.1, f32[3072]{0:T(1024)S(1)} %broadcast_multiply_fusion.1, f32[]{:T(128)} %constant.37.clone.1, pred[3072]{0:T(1024)(128)(4,1)S(1)} %iota_compare_fusion), kind=kCustom, calls=%fused_computation.26 | custom fusion | flops 3932160 | bytes 5272576 | tf_op jit(solution)/shard_map/scatter-add | solution.py:108
  168.8 2.7 convert_element_type.56
  175.4 67.6 %all-reduce.3.cloned.1.call-done = bf16[2048,256]{1,0:T(8,128)(2,1)} async-done(((bf16[2048,256]{1,0:T(8,128)(2,1)}), bf16[2048,256]{1,0:T(8,128)(2,1)}) %all-reduce.3.cloned.1.call-update) | async-done | bytes 1048592 | tf_op jit(solution)/shard_map/psum | solution.py:110
  245.3 34.8 %all-gather.5.cloned.1.call-done = bf16[2048,256]{0,1:T(8,128)(2,1)} async-done(((bf16[256,256]{0,1:T(8,128)(2,1)}), bf16[2048,256]{0,1:T(8,128)(2,1)}) %all-gather.5.cloned.1.call-update) | async-done | bytes 1048592 | tf_op jit(solution)/shard_map/all_gather | solution.py:90
  281.6 16.6 %gather_fusion.3 = bf16[4096,256]{1,0:T(8,128)(2,1)S(1)} fusion(bf16[2048,256]{1,0:T(8,128)(2,1)S(1)} %copy.59, s32[4096]{0:T(1024)} %copy-done.11), kind=kCustom, calls=%fused_computation.3.clone | custom fusion | bytes 4210688 | tf_op jit(solution)/shard_map/jit(_take)/gather | solution.py:91
  300.1 2.9 collective-permute-start.4
  303.0 6.7 %collective-permute-start.5 = (bf16[8,128,256]{2,1,0:T(8,128)(2,1)}, bf16[8,128,256]{2,1,0:T(8,128)(2,1)S(1)}, u32[]{:S(2)}, u32[]{:S(2)}) collective-permute-start(bf16[8,128,256]{2,1,0:T(8,128)(2,1)} %get-tuple-element.14), channel_id=1, source_target_pairs={{0,248},{8,0},{16,8},{24,16},{32,24},{40,32},{48,40},{56,48},{64,5... | collective-permute-start | bytes 1572872 | tf_op jit(solution)/shard_map/ppermute | solution.py:15
  309.7 2.7 collective-permute-start.7
  312.4 2.6 add_convert_fusion.1
  316.1 3.1 fusion.65
  319.3 13.0 %gather_fusion.5 = bf16[3072,256]{1,0:T(8,128)(2,1)} fusion(bf16[2048,256]{1,0:T(8,128)(2,1)S(1)} %copy.59, s32[3072]{0:T(1024)S(1)} %copy-done.15), kind=kCustom, calls=%fused_computation.5.clone | custom fusion | bytes 3158016 | tf_op jit(solution)/shard_map/jit(_take)/gather | solution.py:97
  332.2 10.8 %collective-permute-done.4 = bf16[8,128,256]{2,1,0:T(8,128)(2,1)S(1)} collective-permute-done((bf16[8,128,256]{2,1,0:T(8,128)(2,1)}, bf16[8,128,256]{2,1,0:T(8,128)(2,1)S(1)}, u32[]{:S(2)}, u32[]{:S(2)}) %collective-permute-start.4) | collective-permute-done | bytes 524320 | tf_op jit(solution)/shard_map/ppermute | solution.py:15
  343.0 9.4 %collective-permute-done.5 = bf16[8,128,256]{2,1,0:T(8,128)(2,1)S(1)} collective-permute-done((bf16[8,128,256]{2,1,0:T(8,128)(2,1)}, bf16[8,128,256]{2,1,0:T(8,128)(2,1)S(1)}, u32[]{:S(2)}, u32[]{:S(2)}) %collective-permute-start.5) | collective-permute-done | bytes 524320 | tf_op jit(solution)/shard_map/ppermute | solution.py:15
  356.0 14.7 %gather_fusion.4 = bf16[3072,256]{1,0:T(8,128)(2,1)} fusion(bf16[6144,256]{1,0:T(8,128)(2,1)} %pad_maximum_fusion.1, s32[3072]{0:T(1024)S(1)} %copy-done.13), kind=kCustom, calls=%fused_computation.4.clone | custom fusion | bytes 3158016 | tf_op jit(solution)/shard_map/jit(_take)/gather | solution.py:96
  370.7 3.7 convolution_add_fusion.1
  374.4 5.3 %fusion.130 = (f32[3072]{0:T(1024)S(1)}, f32[3072,256]{0,1:T(8,128)}) fusion(bf16[2,256,256]{2,1,0:T(8,128)(2,1)S(1)} %copy-done.10, f32[3072,256]{1,0:T(8,128)} %convolution_add_fusion.1, bf16[3072,256]{1,0:T(8,128)(2,1)} %gather_fusion.5, f32[256]{0:T(256)S(1)} %bitcast.131, pred[3072]{0:T(1024)(128)(4,1)S(1)} %copy-done.24, bf16[2,768,256]{2,1,0:T(8,128)(2,1)} %param.26), kind=kOutput, calls=%fused_computation.159 | convolution fusion | flops 810021888 | bytes 8142848 | tf_op jit(solution)/shard_map/dot_general | solution.py:39
  383.6 19.3 %scatter_custom_fusion.1 = f32[2048,256]{1,0:T(8,128)} fusion(s32[3072]{0:T(1024)} %param.23, f32[3072,256]{1,0:T(8,128)S(1)} %copy.61, f32[256]{0:T(256)S(1)} %bitcast.128, f32[3072]{0:T(1024)S(1)} %add_rsqrt_fusion, f32[3072]{0:T(1024)S(1)} %broadcast_multiply_fusion, f32[]{:T(128)} %constant.37.clone.1, pred[3072]{0:T(1024)(128)(4,1)S(1)} %iota_compare_fusion), kind=kCustom, calls=%fused_computation.27 | custom fusion | flops 3932160 | bytes 5272576 | tf_op jit(solution)/shard_map/scatter-add | solution.py:108
  402.9 2.7 convert_element_type.65
  406.8 5.3 %add_convert_fusion = bf16[3072,256]{1,0:T(8,128)(2,1)} fusion(bf16[3072,256]{1,0:T(8,128)(2,1)} %copy-done.5, f32[3072,256]{1,0:T(8,128)S(1)} %copy.61, f32[256]{0:T(256)} %bitcast.127, f32[3072]{0:T(1024)} %copy-done.18, f32[3072]{0:T(1024)S(1)} %broadcast_multiply_fusion, pred[3072]{0:T(1024)(128)(4,1)S(1)} %iota_compare_fusion), kind=kLoop, calls=%fused_computation.20 | loop fusion | flops 5505024 | bytes 6320128 | tf_op jit(solution)/shard_map/convert_element_type | solution.py:42
  412.0 63.9 %all-reduce.5.cloned.1.call-done = bf16[2048,256]{1,0:T(8,128)(2,1)} async-done(((bf16[2048,256]{1,0:T(8,128)(2,1)}), bf16[2048,256]{1,0:T(8,128)(2,1)}) %all-reduce.5.cloned.1.call-update) | async-done | bytes 1048592 | tf_op jit(solution)/shard_map/psum | solution.py:110
  (120 shorter events, 39.9 us)
Async XLA Ops:
  7.2 41.0 %all-gather.3.cloned.1.call-start = ((), (), s32[]{:S(2)}) async-start(), calls=%async_computation | async-start | bytes 1179648 | tf_op jit(solution)/shard_map/all_gather | solution.py:90
  7.9 235.1 %all-reduce.3.cloned.1.call-start = ((), (), s32[]{:S(2)}) async-start(), calls=%async_computation.1 | async-start | bytes 2097152 | tf_op jit(solution)/shard_map/psum | solution.py:110
  26.6 109.8 %copy-start.21 = (pred[3072]{0:T(1024)(128)(4,1)}, pred[3072]{0:T(1024)(128)(4,1)S(1)}, u32[]{:S(2)}) copy-start(pred[3072]{0:T(1024)(128)(4,1)S(1)} %compare_and_fusion.2) | copy-start | bytes 9220
  27.3 112.9 %copy-start.23 = (pred[3072]{0:T(1024)(128)(4,1)}, pred[3072]{0:T(1024)(128)(4,1)S(1)}, u32[]{:S(2)}) copy-start(pred[3072]{0:T(1024)(128)(4,1)S(1)} %compare_and_fusion.1) | copy-start | bytes 9220
  28.0 93.7 %copy-start.12 = (s32[3072]{0:T(1024)}, s32[3072]{0:T(1024)S(1)}, u32[]{:S(2)}) copy-start(s32[3072]{0:T(1024)S(1)} %fusion.102) | copy-start | bytes 36868
  28.7 51.8 %copy-start.14 = (s32[3072]{0:T(1024)}, s32[3072]{0:T(1024)S(1)}, u32[]{:S(2)}) copy-start(s32[3072]{0:T(1024)S(1)} %fusion.103) | copy-start | bytes 36868
  28.8 33.7 %copy-start.19 = (pred[8,4,128]{2,1,0:T(4,128)(4,1)}, pred[8,4,128]{2,1,0:T(4,128)(4,1)S(1)}, u32[]{:S(2)}) copy-start(pred[8,4,128]{2,1,0:T(4,128)(4,1)S(1)} %get-tuple-element.11) | copy-start | bytes 12292
  28.8 33.7 %copy-start.11 = (s32[4096]{0:T(1024)}, s32[4096]{0:T(1024)S(1)}, u32[]{:S(2)}) copy-start(s32[4096]{0:T(1024)S(1)} %broadcast_clamp_fusion) | copy-start | bytes 49156
  63.3 13.4 %copy-start.29 = (f32[2,256]{1,0:T(2,128)S(1)}, f32[2,256]{1,0:T(2,128)}, u32[]{:S(2)}) copy-start(f32[2,256]{1,0:T(2,128)} %param.29) | copy-start | bytes 6148
  63.3 14.0 %copy-start.6 = (bf16[3072,256]{1,0:T(8,128)(2,1)S(1)}, bf16[3072,256]{1,0:T(8,128)(2,1)}, u32[]{:S(2)}) copy-start(bf16[3072,256]{1,0:T(8,128)(2,1)} %param.21) | copy-start | bytes 4718596
  64.4 29.0 %collective-permute-start.2 = (bf16[8,128,256]{2,1,0:T(8,128)(2,1)}, bf16[8,128,256]{2,1,0:T(8,128)(2,1)S(1)}, u32[]{:S(2)}, u32[]{:S(2)}) collective-permute-start(bf16[8,128,256]{2,1,0:T(8,128)(2,1)} %get-tuple-element.20), channel_id=1, source_target_pairs={{0,64},{8,72},{16,80},{24,88},{32,96},{40,104},{48,112},{56,120},{... | collective-permute-start | bytes 1572872 | tf_op jit(solution)/shard_map/ppermute | solution.py:15
  65.1 28.4 %collective-permute-start.3 = (bf16[8,128,256]{2,1,0:T(8,128)(2,1)}, bf16[8,128,256]{2,1,0:T(8,128)(2,1)S(1)}, u32[]{:S(2)}, u32[]{:S(2)}) collective-permute-start(bf16[8,128,256]{2,1,0:T(8,128)(2,1)} %get-tuple-element.19), channel_id=1, source_target_pairs={{0,192},{8,200},{16,208},{24,216},{32,224},{40,232},{48,240},{56,2... | collective-permute-start | bytes 1572872 | tf_op jit(solution)/shard_map/ppermute | solution.py:15
  67.1 44.4 %collective-permute-start = (bf16[8,128,256]{2,1,0:T(8,128)(2,1)S(1)}, bf16[8,128,256]{2,1,0:T(8,128)(2,1)}, u32[]{:S(2)}, u32[]{:S(2)}) collective-permute-start(bf16[8,128,256]{2,1,0:T(8,128)(2,1)S(1)} %get-tuple-element.17), channel_id=1, source_target_pairs={{0,8},{8,16},{16,24},{24,32},{32,40},{40,48},{48,56},{56,64},{64,7... | collective-permute-start | bytes 1572872 | tf_op jit(solution)/shard_map/ppermute | solution.py:15
  71.9 46.3 %collective-permute-start.1 = (bf16[8,128,256]{2,1,0:T(8,128)(2,1)S(1)}, bf16[8,128,256]{2,1,0:T(8,128)(2,1)}, u32[]{:S(2)}, u32[]{:S(2)}) collective-permute-start(bf16[8,128,256]{2,1,0:T(8,128)(2,1)S(1)} %get-tuple-element.18), channel_id=1, source_target_pairs={{0,248},{8,0},{16,8},{24,16},{32,24},{40,32},{48,40},{56,48},{64,5... | collective-permute-start | bytes 1572872 | tf_op jit(solution)/shard_map/ppermute | solution.py:15
  77.3 71.5 %copy-start.26 = (f32[1,256]{1,0:T(1,128)}, f32[1,256]{1,0:T(1,128)S(1)}, u32[]{:S(2)}) copy-start(f32[1,256]{1,0:T(1,128)S(1)} %get-tuple-element.26) | copy-start | bytes 3076
  121.7 14.7 %copy-start.4 = (f32[3072,256]{1,0:T(8,128)S(1)}, f32[3072,256]{1,0:T(8,128)}, u32[]{:S(2)}) copy-start(f32[3072,256]{1,0:T(8,128)} %fusion.76) | copy-start | bytes 9437188
  136.4 3.7 copy-start.10
  147.8 21.0 %copy-start.1 = (f32[3072,256]{1,0:T(8,128)}, f32[3072,256]{1,0:T(8,128)S(1)}, u32[]{:S(2)}) copy-start(f32[3072,256]{1,0:T(8,128)S(1)} %copy.53) | copy-start | bytes 9437188
  171.5 108.6 %all-gather.5.cloned.1.call-start = ((), (), s32[]{:S(2)}) async-start(), calls=%async_computation.2 | async-start | bytes 1179648 | tf_op jit(solution)/shard_map/all_gather | solution.py:90
  245.3 230.7 %all-reduce.5.cloned.1.call-start = ((), (), s32[]{:S(2)}) async-start(), calls=%async_computation.3 | async-start | bytes 2097152 | tf_op jit(solution)/shard_map/psum | solution.py:110
  281.6 16.6 %copy-start.20 = (pred[8,4,128]{2,1,0:T(4,128)(4,1)S(1)}, pred[8,4,128]{2,1,0:T(4,128)(4,1)}, u32[]{:S(2)}) copy-start(pred[8,4,128]{2,1,0:T(4,128)(4,1)} %copy-done.19) | copy-start | bytes 12292
  298.2 14.2 %copy-start.7 = (bf16[3072,256]{1,0:T(8,128)(2,1)S(1)}, bf16[3072,256]{1,0:T(8,128)(2,1)}, u32[]{:S(2)}) copy-start(bf16[3072,256]{1,0:T(8,128)(2,1)} %param.21) | copy-start | bytes 4718596
  299.0 13.4 %copy-start.2 = (f32[3072,256]{1,0:T(8,128)S(1)}, f32[3072,256]{1,0:T(8,128)}, u32[]{:S(2)}) copy-start(f32[3072,256]{1,0:T(8,128)} %copy-done.1) | copy-start | bytes 9437188
  299.0 13.4 %copy-start.17 = (f32[3072]{0:T(1024)S(1)}, f32[3072]{0:T(1024)}, u32[]{:S(2)}) copy-start(f32[3072]{0:T(1024)} %copy-done.16) | copy-start | bytes 36868
  299.0 13.4 %copy-start.27 = (f32[1,256]{1,0:T(1,128)S(1)}, f32[1,256]{1,0:T(1,128)}, u32[]{:S(2)}) copy-start(f32[1,256]{1,0:T(1,128)} %copy-done.26) | copy-start | bytes 3076
  300.1 42.9 %collective-permute-start.4 = (bf16[8,128,256]{2,1,0:T(8,128)(2,1)}, bf16[8,128,256]{2,1,0:T(8,128)(2,1)S(1)}, u32[]{:S(2)}, u32[]{:S(2)}) collective-permute-start(bf16[8,128,256]{2,1,0:T(8,128)(2,1)} %get-tuple-element.13), channel_id=1, source_target_pairs={{0,8},{8,16},{16,24},{24,32},{32,40},{40,48},{48,56},{56,64},{64,7... | collective-permute-start | bytes 1572872 | tf_op jit(solution)/shard_map/ppermute | solution.py:15
  303.0 49.4 %collective-permute-start.5 = (bf16[8,128,256]{2,1,0:T(8,128)(2,1)}, bf16[8,128,256]{2,1,0:T(8,128)(2,1)S(1)}, u32[]{:S(2)}, u32[]{:S(2)}) collective-permute-start(bf16[8,128,256]{2,1,0:T(8,128)(2,1)} %get-tuple-element.14), channel_id=1, source_target_pairs={{0,248},{8,0},{16,8},{24,16},{32,24},{40,32},{48,40},{56,48},{64,5... | collective-permute-start | bytes 1572872 | tf_op jit(solution)/shard_map/ppermute | solution.py:15
  309.7 42.8 %collective-permute-start.6 = (bf16[8,128,256]{2,1,0:T(8,128)(2,1)S(1)}, bf16[8,128,256]{2,1,0:T(8,128)(2,1)}, u32[]{:S(2)}, u32[]{:S(2)}) collective-permute-start(bf16[8,128,256]{2,1,0:T(8,128)(2,1)S(1)} %get-tuple-element.16), channel_id=1, source_target_pairs={{0,64},{8,72},{16,80},{24,88},{32,96},{40,104},{48,112},{56,120},{... | collective-permute-start | bytes 1572872 | tf_op jit(solution)/shard_map/ppermute | solution.py:15
  309.7 42.8 %collective-permute-start.7 = (bf16[8,128,256]{2,1,0:T(8,128)(2,1)S(1)}, bf16[8,128,256]{2,1,0:T(8,128)(2,1)}, u32[]{:S(2)}, u32[]{:S(2)}) collective-permute-start(bf16[8,128,256]{2,1,0:T(8,128)(2,1)S(1)} %get-tuple-element.15), channel_id=1, source_target_pairs={{0,192},{8,200},{16,208},{24,216},{32,224},{40,232},{48,240},{56,2... | collective-permute-start | bytes 1572872 | tf_op jit(solution)/shard_map/ppermute | solution.py:15
  356.0 14.7 %copy-start.3 = (f32[3072,256]{1,0:T(8,128)S(1)}, f32[3072,256]{1,0:T(8,128)}, u32[]{:S(2)}) copy-start(f32[3072,256]{1,0:T(8,128)} %fusion.65) | copy-start | bytes 9437188
  356.0 14.7 %copy-start.22 = (pred[3072]{0:T(1024)(128)(4,1)S(1)}, pred[3072]{0:T(1024)(128)(4,1)}, u32[]{:S(2)}) copy-start(pred[3072]{0:T(1024)(128)(4,1)} %copy-done.21) | copy-start | bytes 9220
  370.7 3.7 copy-start.24
  (10 other events, 21.5 us)
Sparse Core Ops, SparseCore 0:
  9.8 38.3 all-gather.2
  171.7 71.2 all-reduce.2
  245.4 34.7 all-gather.4
  405.7 70.1 all-reduce.4
where the time goes:
time: 488 us; the launch traced here: 486 us
  waiting for transfers between devices  231 us (47%)
  local copies, waits for them, and re-layouts  103 us (21%)
  other arithmetic  66.4 us (14%)
  matrix products  29.4 us (6%)
  starting transfers between devices  24.7 us (5%)
  blocking collectives  15.9 us (3%)
  between operations  14.8 us (3%)
    psum x2, waiting for transfers between devices, shards(): lax.psum(domain_sum.astype(jnp.bfloat16), 'edge').astype(jnp.float32)  131 us
    all_gather x2, waiting for transfers between devices, shards(): domain_rows = lax.all_gather(owned_rows, 'edge', axis=0, tiled=True)  54.2 us
    ppermute x8, waiting for transfers between devices, passed_along(): return lax.ppermute(value, axis, pairs)  45 us
    scatter-add x2, other arithmetic, shards(): jax.ops.segment_sum(messages, receivers, num_segments=node_count * rank_c...  38.6 us
    gather x2, local copies, waits for them, and re-layouts, shards(): face_rows = jnp.take(domain_rows, lists_all, axis=0)  30.9 us
    gather x2, local copies, waits for them, and re-layouts, shards(): sender_rows = jnp.take(node_table, senders, axis=0)  29.3 us
    gather x2, local copies, waits for them, and re-layouts, shards(): receiver_rows = jnp.take(domain_rows, receivers, axis=0)  26 us
    ppermute x8, starting transfers between devices, passed_along(): return lax.ppermute(value, axis, pairs)  24.5 us
  transfers between devices with their start and end apart: 12, of which 8 were waited for; matrix products, arithmetic and copies ran while one was open for 10% of the time, Pallas kernels for 0%

commit v1 on v0

v1 whole, which is shorter than its diff:
```python
import functools

import jax
import jax.numpy as jnp
from jax import lax
from jax.experimental import pallas as pl
from jax.experimental.pallas import tpu as pltpu
from jax.sharding import PartitionSpec as P

LAYERS = 2
EPS = 1e-05
FACES = 4
HALO = 128
GROUP = 32
MESH = pl.DeviceIdType.MESH
BF16 = jnp.bfloat16
F32 = jnp.float32


def dot(a, b):
    return jnp.dot(a, b, preferred_element_type=F32)


def layer_norm(values, gain):
    center = values - jnp.mean(values, axis=-1, keepdims=True)
    spread = jnp.mean(center * center, axis=-1, keepdims=True)
    return center * lax.rsqrt(spread + EPS) * gain


def edge_kernel(
    live_ref,
    send_ref,
    recv_ref,
    recv_row_ref,
    table_ref,
    edge_ref,
    w1_ref,
    b1_ref,
    w2_ref,
    gain_ref,
    edge_out_ref,
    part_ref,
    s_ref,
    r_ref,
    pre_ref,
    msg_ref,
):
    nodes = part_ref.shape[0]
    rows = table_ref.shape[0]
    edges, width = edge_ref.shape
    half = width // 2
    step = 512
    chunk = 256

    @pl.loop(0, rows // step)
    def _(i):
        base = pl.multiple_of(i * step, step)
        val = dot(table_ref[pl.ds(base, step), :], w1_ref[width : 2 * width, :])
        s_ref[pl.ds(2 * base, step, stride=2), :] = val[:, :half]
        s_ref[pl.ds(2 * base + 1, step, stride=2), :] = val[:, half:]

    @pl.loop(0, nodes // step)
    def _(i):
        base = pl.multiple_of(i * step, step)
        val = dot(table_ref[pl.ds(base, step), :], w1_ref[2 * width :, :]) + b1_ref[...]
        r_ref[pl.ds(2 * base, step, stride=2), :] = val[:, :half]
        r_ref[pl.ds(2 * base + 1, step, stride=2), :] = val[:, half:]

    live = live_ref[0, 0]

    @pl.loop(0, edges // chunk)
    def _(i):
        base = pl.multiple_of(i * chunk, chunk)

        @pl.loop(0, chunk // GROUP)
        def _(g):
            for u in range(GROUP):
                k = base + g * GROUP + u
                a = send_ref[k]
                b = recv_ref[k]
                at = pl.multiple_of(g * (2 * GROUP), 2 * GROUP) + 2 * u
                pre_ref[pl.ds(at, 2), :] = (
                    s_ref[pl.ds(pl.multiple_of(2 * a, 2), 2), :]
                    + r_ref[pl.ds(pl.multiple_of(2 * b, 2), 2), :]
                )

        old = edge_ref[pl.ds(base, chunk), :]
        pre = dot(old, w1_ref[:width, :])
        low = pre[:, :half] + pre_ref[pl.ds(0, chunk, stride=2), :]
        high = pre[:, half:] + pre_ref[pl.ds(1, chunk, stride=2), :]
        hidden = jnp.maximum(jnp.concatenate([low, high], axis=1), 0.0).astype(BF16)
        message = layer_norm(dot(hidden, w2_ref[...]), gain_ref[...])
        slot = lax.broadcasted_iota(jnp.int32, (chunk, 1), 0) + base
        message = jnp.where(slot < live, message, 0.0)
        edge_out_ref[pl.ds(base, chunk), :] = (old.astype(F32) + message).astype(BF16)
        msg_ref[pl.ds(base, chunk), :] = message.astype(BF16)

    nb = 256
    kb = 512

    @pl.loop(0, nodes // nb)
    def _(i):
        base = pl.multiple_of(i * nb, nb)
        ids = lax.broadcasted_iota(jnp.int32, (nb, kb), 0) + base
        acc = jnp.zeros((nb, width), F32)
        for j in range(edges // kb):
            hit = ids == recv_row_ref[:, j * kb : (j + 1) * kb]
            acc = acc + dot(
                jnp.where(hit, 1.0, 0.0).astype(BF16), msg_ref[j * kb : (j + 1) * kb, :]
            )
        part_ref[pl.ds(base, nb), :] = acc.astype(BF16)


def edge_step(table, edges, senders, receivers, live, w1, b1, w2, gain, nodes):
    vmem = pl.BlockSpec(memory_space=pltpu.VMEM)
    smem = pl.BlockSpec(memory_space=pltpu.SMEM)
    rows, width = table.shape
    count = edges.shape[0]
    return pl.pallas_call(
        edge_kernel,
        out_shape=(
            jax.ShapeDtypeStruct(edges.shape, BF16),
            jax.ShapeDtypeStruct((nodes, width), BF16),
        ),
        in_specs=[smem, smem, smem] + [vmem] * 7,
        out_specs=(vmem, vmem),
        scratch_shapes=[
            pltpu.VMEM((2 * rows, width // 2), F32),
            pltpu.VMEM((2 * nodes, width // 2), F32),
            pltpu.VMEM((2 * 256, width // 2), F32),
            pltpu.VMEM((count, width), BF16),
        ],
        compiler_params=pltpu.CompilerParams(vmem_limit_bytes=48 * 2**20),
        cost_estimate=pl.CostEstimate(
            flops=12 * 10**9, bytes_accessed=9 * 2**20, transcendentals=0
        ),
        name="edge_step",
    )(live, senders, receivers, receivers.reshape(1, -1), table, edges, w1, b1, w2, gain)


def node_kernel(reduce, spread, *refs):
    refs = list(refs)
    own_ref = refs.pop(0)
    if reduce:
        part_ref, w1_ref, b1_ref, w2_ref, gain_ref = (refs.pop(0) for _ in range(5))
    if spread:
        list_ref = refs.pop(0)
    if reduce:
        node_out_ref = refs.pop(0)
    if spread:
        table_ref = refs.pop(0)
    if reduce:
        pair_ref, sums_ref, got_ref = (refs.pop(0) for _ in range(3))
        pair_sem, sum_sem = (refs.pop(0) for _ in range(2))
    if spread:
        lists_ref, zface_ref, xface_ref = (refs.pop(0) for _ in range(3))
        list_sem, node_sem, zf_sem, xf_sem, fn_sem, fz_sem, fx_sem = (
            refs.pop(0) for _ in range(7)
        )

    d = lax.axis_index("dom")
    e = lax.axis_index("edge")
    doms = lax.axis_size("dom")
    count = lax.axis_size("edge")
    chips = count // 2
    stride = doms // 4
    size, width = own_ref.shape
    q = e // 2
    c = e % 2
    sib = 2 * q + 1 - c

    def peer(t):
        return 2 * ((q + t) % chips) + c

    def source(t):
        return 2 * ((q - t + chips) % chips) + c

    offsets = (1, doms - 1, stride, doms - stride)
    there = [(d + s) % doms for s in offsets]

    barrier = pltpu.get_barrier_semaphore()
    greet = [(d, sib)] + [(d, peer(t)) for t in range(1, chips)]
    if spread:
        greet += [(there[f], peer(t)) for f in range(2) for t in range(chips)]
        greet += [(there[f], e) for f in range(2, 4)]
    for who in greet:
        pl.semaphore_signal(barrier, inc=1, device_id=who, device_id_type=MESH)
    pl.semaphore_wait(barrier, len(greet))

    def send(src, dst, sems, index, who):
        copy = pltpu.make_async_remote_copy(
            src_ref=src,
            dst_ref=dst,
            send_sem=sems.at[(0,) + index],
            recv_sem=sems.at[(1,) + index],
            device_id=who,
            device_id_type=MESH,
        )
        copy.start()
        return copy

    sent = []
    own = own_ref[...]

    if spread:
        lists_ref[0] = list_ref[...]
        got_lists = [None]
        for t in range(1, chips):
            copy = send(list_ref, lists_ref.at[t], list_sem, (t,), (d, peer(t)))
            got_lists.append(copy)

    if reduce:
        pairs = []
        for t in range(chips - 1, -1, -1):
            block = 2 * ((q + t) % chips) + 1 - c
            copy = send(
                part_ref.at[pl.ds(pl.multiple_of(block * size, size), size), :],
                pair_ref.at[t],
                pair_sem,
                (t,),
                (d, sib),
            )
            pairs.append((t, copy))
        moved = []
        mine = None
        for t, copy in pairs:
            copy.wait_recv()
            at = pl.multiple_of(peer(t) * size, size)
            total = part_ref[pl.ds(at, size), :].astype(F32) + pair_ref[t].astype(F32)
            if t:
                sums_ref[t] = total.astype(BF16)
                moved.append(send(sums_ref.at[t], got_ref.at[t], sum_sem, (t,), (d, peer(t))))
            else:
                mine = total
            sent.append(copy)
        pre = dot(own, w1_ref[:width, :]) + b1_ref[...]
        for t, copy in zip(range(chips - 1, 0, -1), moved):
            copy.wait_recv()
            mine = mine + got_ref[t].astype(F32)
            sent.append(copy)
        pre = pre + dot(mine.astype(BF16), w1_ref[width:, :])
        hidden = jnp.maximum(pre, 0.0).astype(BF16)
        update = layer_norm(dot(hidden, w2_ref[...]), gain_ref[...])
        own = (own.astype(F32) + update).astype(BF16)
        node_out_ref[...] = own

    if spread:
        nodes = count * size

        def node_at(owner):
            return table_ref.at[pl.ds(pl.multiple_of(owner * size, size), size), :]

        def halo_at(owner, f):
            at = nodes + (owner * FACES + f) * HALO
            return table_ref.at[pl.ds(pl.multiple_of(at, HALO), HALO), :]

        table_ref[pl.ds(pl.multiple_of(e * size, size), size), :] = own
        node_copies = {}
        for t in (2, 1, 3, 0):
            who = (d, peer(t)) if t else (d, sib)
            node_copies[t] = send(node_at(e), node_at(e), node_sem, (t,), who)

        ids = lax.broadcasted_iota(jnp.int32, (size, HALO), 0)

        def picked(values, row):
            hit = jnp.where(ids == row, 1.0, 0.0).astype(BF16)
            return lax.dot_general(
                hit, values, (((0,), (0,)), ((), ())), preferred_element_type=F32
            ).astype(BF16)

        z_copies = {}
        for f in range(2):
            zface_ref[f] = picked(own, lists_ref[0, f : f + 1, :])
            for t in (2, 1, 3, 0):
                z_copies[f, t] = send(
                    zface_ref.at[f], halo_at(e, f), zf_sem, (f, t), (there[f], peer(t))
                )
        x_copies = {}
        forwards = []
        for t in range(chips):
            owner = source(t)
            if t:
                node_copies[t].wait_recv()
                forwards.append(send(node_at(owner), node_at(owner), fn_sem, (t,), (d, sib)))
                got_lists[t].wait_recv()
            values = node_ref_load(table_ref, owner, size)
            for f in range(2, 4):
                xface_ref[t, f - 2] = picked(values, lists_ref[t, f : f + 1, :])
                x_copies[f - 2, t] = send(
                    xface_ref.at[t, f - 2],
                    halo_at(owner, f),
                    xf_sem,
                    (f - 2, t),
                    (there[f], e),
                )
        for t in range(chips):
            for f in range(2):
                x_copies[f, t].wait_recv()
                place = halo_at(source(t), f + 2)
                forwards.append(send(place, place, fx_sem, (f, t), (d, sib)))
        for t in range(chips):
            for f in range(2):
                z_copies[f, t].wait_recv()
                place = halo_at(source(t), f)
                forwards.append(send(place, place, fz_sem, (f, t), (d, sib)))
        node_copies[0].wait_recv()
        for copy in forwards:
            copy.wait()
        for copy in got_lists[1:] + list(node_copies.values()):
            copy.wait_send()
        for copy in list(z_copies.values()) + list(x_copies.values()):
            copy.wait_send()
    for copy in sent:
        copy.wait_send()


def node_ref_load(table_ref, owner, size):
    return table_ref[pl.ds(pl.multiple_of(owner * size, size), size), :]


def node_step(own, reduce=None, lists=None, collective_id=0):
    vmem = pl.BlockSpec(memory_space=pltpu.VMEM)
    size, width = own.shape
    count = lax.axis_size("edge")
    chips = count // 2
    dma = pltpu.SemaphoreType.DMA
    args, outs, scratch = [own], [], []
    if reduce is not None:
        args += list(reduce)
        outs.append(jax.ShapeDtypeStruct(own.shape, BF16))
    if lists is not None:
        args.append(lists)
        rows = count * (size + FACES * HALO)
        outs.append(jax.ShapeDtypeStruct((rows, width), BF16))
    if reduce is not None:
        scratch += [pltpu.VMEM((chips, size, width), BF16)] * 3
        scratch += [dma((2, chips)), dma((2, chips))]
    if lists is not None:
        scratch += [
            pltpu.VMEM((chips, FACES, HALO), jnp.int32),
            pltpu.VMEM((2, HALO, width), BF16),
            pltpu.VMEM((chips, 2, HALO, width), BF16),
        ]
        scratch += [dma((2, chips)), dma((2, chips)), dma((2, 2, chips)), dma((2, 2, chips))]
        scratch += [dma((2, chips)), dma((2, 2, chips)), dma((2, 2, chips))]
    return pl.pallas_call(
        functools.partial(node_kernel, reduce is not None, lists is not None),
        out_shape=tuple(outs),
        in_specs=[vmem] * len(args),
        out_specs=(vmem,) * len(outs),
        scratch_shapes=scratch,
        compiler_params=pltpu.CompilerParams(
            collective_id=collective_id, has_side_effects=True, vmem_limit_bytes=48 * 2**20
        ),
        cost_estimate=pl.CostEstimate(flops=10**8, bytes_accessed=8 * 2**20, transcendentals=0),
        name="node_step",
    )(*args)


def shards(
    node_lat,
    edge_lat,
    senders,
    receivers,
    live_edges,
    send_rows,
    edge_w1,
    edge_b1,
    edge_w2,
    edge_gain,
    node_w1,
    node_b1,
    node_w2,
    node_gain,
):
    lists = send_rows[0]
    nodes = node_lat.shape[0] * lax.axis_size("edge")
    own, edges = node_lat, edge_lat
    (table,) = node_step(own, lists=lists, collective_id=0)
    for l in range(LAYERS):
        edges, part = edge_step(
            table,
            edges,
            senders,
            receivers,
            live_edges,
            edge_w1[l],
            edge_b1[l : l + 1],
            edge_w2[l],
            edge_gain[l : l + 1],
            nodes,
        )
        sums = (part, node_w1[l], node_b1[l : l + 1], node_w2[l], node_gain[l : l + 1])
        if l < LAYERS - 1:
            own, table = node_step(own, sums, lists, collective_id=1 + l)
        else:
            (own,) = node_step(own, sums, None, collective_id=1 + l)
    return (own, edges)


def solution(mesh):
    rows = P(("dom", "edge"), None)
    in_specs = (
        rows,
        rows,
        P(("dom", "edge")),
        P(("dom", "edge")),
        P("dom", "edge"),
        P(("dom", "edge"), None, None),
    ) + (P(),) * 8
    return jax.shard_map(
        shards, mesh=mesh, in_specs=in_specs, out_specs=(rows, rows), check_vma=False
    )
```

time: 488 us -> 163 us (0.33)
  waiting for transfers between devices: 231 us -> 0 us
  Pallas kernels: 0 us -> 153 us
  local copies, waits for them, and re-layouts: 103 us -> 8.67 us
  other arithmetic: 66.4 us -> 0 us
  matrix products: 29.4 us -> 0 us
  starting transfers between devices: 24.7 us -> 0 us
  blocking collectives: 15.9 us -> 0 us
  between operations: 14.8 us -> 1.49 us
    pallas_call x0 -> x5, Pallas kernels: none -> 153 us  [the longest x3 107 us: node_step(): pl.pallas_call(functools.partial(node_kernel, reduce is not None, lists i...]
    psum x2 -> x0, waiting for transfers between devices: 131 us -> none  [shards(): lax.psum(domain_sum.astype(jnp.bfloat16), 'edge').astype(jnp.float32)]
    gather x6 -> x0, local copies, waits for them, and re-layouts: 86.2 us -> none  [the longest x2 30.9 us: shards(): face_rows = jnp.take(domain_rows, lists_all, axis=0)]
    all_gather x2 -> x0, waiting for transfers between devices: 54.2 us -> none  [shards(): domain_rows = lax.all_gather(owned_rows, 'edge', axis=0, tiled=True)]
    ppermute x8 -> x0, waiting for transfers between devices: 45 us -> none  [passed_along(): return lax.ppermute(value, axis, pairs)]
    scatter-add x2 -> x0, other arithmetic: 38.6 us -> none  [shards(): jax.ops.segment_sum(messages, receivers, num_segments=node_count * rank_c...]
    dot_general x10 -> x0, matrix products: 29.4 us -> none  [the longest x2 10.6 us: edge_update(): jnp.dot(hidden_rows, weight_out, preferred_element_type=jnp.float32)]
    ppermute x8 -> x0, starting transfers between devices: 24.5 us -> none  [passed_along(): return lax.ppermute(value, axis, pairs)]
  transfers between devices with their start and end apart: 12 -> 0, of which waited for: 8 -> 0; matrix products, arithmetic and copies ran while one was open for 10% -> 0% of each run, Pallas kernels for 0% -> 0%
where the time goes in v1:
time: 163 us
  Pallas kernels  153 us (94%)
  local copies, waits for them, and re-layouts  8.67 us (5%)
    pallas_call x3, Pallas kernels, node_step(): pl.pallas_call(functools.partial(node_kernel, reduce is not None, lists i...  107 us
    pallas_call x2, Pallas kernels, edge_step(): pl.pallas_call(edge_kernel, out_shape=(jax.ShapeDtypeStruct(edges.shape,...  45.6 us
    unnamed x17, local copies, waits for them, and re-layouts  3.99 us

profile of v1, /device:TPU:1, one launch (start us, length us, event | category | flops | bytes accessed | tf_op | source)
XLA Modules:
  0.0 162.9 jit_solution(153624621984379999)
XLA Ops:
  0.6 0.0 copy-start.7
  1.4 0.8 fusion.2
  2.1 0.8 fusion
  2.9 1.0 slice_bitcast_fusion.5
  3.9 0.0 copy-start.1
  3.9 0.0 copy-start.2
  3.9 1.0 slice_bitcast_fusion.4
  5.0 1.1 slice_bitcast_fusion.2
  6.0 0.0 copy-done.7
  6.0 0.1 slice_bitcast_fusion
  6.1 0.0 copy-done.1
  6.1 0.0 copy-done.2
  6.1 0.0 copy-start.4
  6.1 0.0 copy-start.5
  6.1 0.0 copy-start.6
  6.1 38.6 %node_step.3.table_ref = bf16[6144,256]{1,0:T(8,128)(2,1)S(1)} custom-call(bf16[256,256]{1,0:T(8,128)(2,1)S(1)} %copy-done.1, s32[4,128]{1,0:T(4,128)S(1)} %bitcast.18), custom_call_target="tpu_custom_call" | custom-call | flops 100000000 | bytes 8388608 | tf_op jit(solution)/shard_map/node_step/pallas_call | solution.py:346
  44.7 0.0 copy-start
  44.7 1.6 %copy-done = bf16[6144,256]{1,0:T(8,128)(2,1)} copy-done((bf16[6144,256]{1,0:T(8,128)(2,1)}, bf16[6144,256]{1,0:T(8,128)(2,1)S(1)}, u32[]{:S(2)}) %copy-start) | copy-done | bytes 3145752
  46.4 0.0 copy-done.4
  46.4 0.0 copy-done.5
  46.4 0.0 copy-done.6
  46.4 22.5 %edge_step.2 = (bf16[3072,256]{1,0:T(8,128)(2,1)S(1)}, bf16[2048,256]{1,0:T(8,128)(2,1)S(1)}) custom-call(s32[1,1]{1,0:T(1,128)S(6)} %copy.17.live_ref, s32[3072]{0:T(1024)S(1)} %copy-done.5, s32[3072]{0:T(1024)S(1)} %copy-done.6, s32[1,3072]{1,0:T(1,128)S(1)} %bitcast.20, bf16[6144,256]{1,0:T(8,128)(2,1)} %copy-done, bf16[3072,256]{1,0:T(8,128)(2,1)S(1)} %copy-done.4, ...), custom_call_target="tpu_custom_call" | custom-call | flops 12000000000 | bytes 9437184 | tf_op jit(solution)/shard_map/edge_step/pallas_call | solution.py:119
  68.9 52.0 %node_step.4 = (bf16[256,256]{1,0:T(8,128)(2,1)S(1)}, bf16[6144,256]{1,0:T(8,128)(2,1)S(1)}) custom-call(bf16[256,256]{1,0:T(8,128)(2,1)S(1)} %copy-done.1, bf16[2048,256]{1,0:T(8,128)(2,1)S(1)} %get-tuple-element.8.refs_1_, bf16[512,256]{1,0:T(8,128)(2,1)S(1)} %get-tuple-element.17.refs_2_, f32[1,256]{1,0:T(1,128)S(1)} %get-tuple-element.32.refs_3_, ...), custom_call_target="tpu_custom_call" | custom-call | flops 100000000 | bytes 8388608 | tf_op jit(solution)/shard_map/node_step/pallas_call | solution.py:346
  120.9 0.0 copy-start.3
  120.9 1.6 %copy-done.3 = bf16[6144,256]{1,0:T(8,128)(2,1)} copy-done((bf16[6144,256]{1,0:T(8,128)(2,1)}, bf16[6144,256]{1,0:T(8,128)(2,1)S(1)}, u32[]{:S(2)}) %copy-start.3) | copy-done | bytes 3145752
  122.6 23.1 %edge_step.3 = (bf16[3072,256]{1,0:T(8,128)(2,1)}, bf16[2048,256]{1,0:T(8,128)(2,1)S(1)}) custom-call(s32[1,1]{1,0:T(1,128)S(6)} %copy.17.live_ref, s32[3072]{0:T(1024)S(1)} %copy-done.5, s32[3072]{0:T(1024)S(1)} %copy-done.6, s32[1,3072]{1,0:T(1,128)S(1)} %bitcast.21, bf16[6144,256]{1,0:T(8,128)(2,1)} %copy-done.3, ...), custom_call_target="tpu_custom_call" | custom-call | flops 12000000000 | bytes 9437184 | tf_op jit(solution)/shard_map/edge_step/pallas_call | solution.py:119
  145.7 16.6 %node_step.5 = bf16[256,256]{1,0:T(8,128)(2,1)S(1)} custom-call(bf16[256,256]{1,0:T(8,128)(2,1)S(1)} %get-tuple-element.9.refs_0_, bf16[2048,256]{1,0:T(8,128)(2,1)S(1)} %get-tuple-element.12.refs_1_, bf16[512,256]{1,0:T(8,128)(2,1)S(1)} %get-tuple-element.16.refs_2_, f32[1,256]{1,0:T(1,128)S(1)} %get-tuple-element.33.refs_3_, ...), custom_call_target="tpu_custom_call" | custom-call | flops 100000000 | bytes 8388608 | tf_op jit(solution)/shard_map/node_step/pallas_call | solution.py:346
  162.3 0.7 copy.18
Async XLA Ops:
  0.6 5.4 %copy-start.7 = (bf16[2,768,256]{2,1,0:T(8,128)(2,1)S(1)}, bf16[2,768,256]{2,1,0:T(8,128)(2,1)}, u32[]{:S(2)}) copy-start(bf16[2,768,256]{2,1,0:T(8,128)(2,1)} %param.20) | copy-start | bytes 2359300
  3.9 2.2 %copy-start.1 = (bf16[256,256]{1,0:T(8,128)(2,1)S(1)}, bf16[256,256]{1,0:T(8,128)(2,1)}, u32[]{:S(2)}) copy-start(bf16[256,256]{1,0:T(8,128)(2,1)} %refs_0_.3) | copy-start | bytes 393220
  3.9 2.2 %copy-start.2 = (s32[1,4,128]{2,1,0:T(4,128)S(1)}, s32[1,4,128]{2,1,0:T(4,128)}, u32[]{:S(2)}) copy-start(s32[1,4,128]{2,1,0:T(4,128)} %param.19) | copy-start | bytes 6148
  6.1 40.3 %copy-start.4 = (bf16[3072,256]{1,0:T(8,128)(2,1)S(1)}, bf16[3072,256]{1,0:T(8,128)(2,1)}, u32[]{:S(2)}) copy-start(bf16[3072,256]{1,0:T(8,128)(2,1)} %edge_ref.1) | copy-start | bytes 4718596
  6.1 40.3 %copy-start.5 = (s32[3072]{0:T(1024)S(1)}, s32[3072]{0:T(1024)}, u32[]{:S(2)}) copy-start(s32[3072]{0:T(1024)} %send_ref.3) | copy-start | bytes 36868
  6.1 40.2 %copy-start.6 = (s32[3072]{0:T(1024)S(1)}, s32[3072]{0:T(1024)}, u32[]{:S(2)}) copy-start(s32[3072]{0:T(1024)} %recv_ref.3) | copy-start | bytes 36868
  44.7 1.7 %copy-start = (bf16[6144,256]{1,0:T(8,128)(2,1)}, bf16[6144,256]{1,0:T(8,128)(2,1)S(1)}, u32[]{:S(2)}) copy-start(bf16[6144,256]{1,0:T(8,128)(2,1)S(1)} %node_step.3.table_ref) | copy-start | bytes 9437188
  120.9 1.7 %copy-start.3 = (bf16[6144,256]{1,0:T(8,128)(2,1)}, bf16[6144,256]{1,0:T(8,128)(2,1)S(1)}, u32[]{:S(2)}) copy-start(bf16[6144,256]{1,0:T(8,128)(2,1)S(1)} %get-tuple-element.10.table_ref) | copy-start | bytes 9437188

commit v2 on v0

v2 whole, which is shorter than its diff:
```python
import jax
import jax.numpy as jnp
from jax import lax
from jax.experimental import pallas as pl
from jax.experimental.pallas import tpu as pltpu
from jax.sharding import PartitionSpec as P

LAYERS = 2
EPS = 1e-05
FACES = 4
HALO = 128
GROUP = 64
CHUNK = 1536
STEP = 1024
MESH = pl.DeviceIdType.MESH
BF16 = jnp.bfloat16
F32 = jnp.float32
UP, DOWN, SIDE, ACROSS = range(4)
REACH = ({0, 1, 2, 3}, {1, 2, 3}, {3})


def dot(a, b):
    return jnp.dot(a, b, preferred_element_type=F32)


def layer_norm(values, gain):
    center = values - jnp.mean(values, axis=-1, keepdims=True)
    spread = jnp.mean(center * center, axis=-1, keepdims=True)
    return center * lax.rsqrt(spread + EPS) * gain


def rows(start, size):
    return pl.ds(pl.multiple_of(start, size), size)


def kernel(
    own_ref,
    edge_ref,
    send_ref,
    recv_ref,
    recv_row_ref,
    live_ref,
    list_ref,
    ew1_ref,
    eb1_ref,
    ew2_ref,
    eg_ref,
    nw1_ref,
    nb1_ref,
    nw2_ref,
    ng_ref,
    node_out_ref,
    edge_out_ref,
    table_ref,
    face_ref,
    lists_ref,
    mid_ref,
    s_ref,
    r_ref,
    pre_ref,
    msg_ref,
    part_ref,
    pair_ref,
    sums_ref,
    got_ref,
    block_send,
    block_recv,
    list_sem,
    pair_sem,
    sum_sem,
):
    d = lax.axis_index("dom")
    e = lax.axis_index("edge")
    doms = lax.axis_size("dom")
    count = lax.axis_size("edge")
    chips = count // 2
    last = chips - 1
    stride = doms // 4
    size, width = own_ref.shape
    half = width // 2
    edges = edge_ref.shape[0]
    nodes = count * size
    parts = size // HALO
    q = e // 2
    c = e % 2
    sib = (d, 2 * q + 1 - c)
    ups = (d, e + 2)
    downs = (d, e - 2)
    there = [(d + s) % doms for s in (1, doms - 1, stride, doms - stride)]

    def peer(t):
        return 2 * ((q + t) % chips) + c

    barrier = pltpu.get_barrier_semaphore()

    def greet(who):
        pl.semaphore_signal(barrier, inc=1, device_id=who, device_id_type=MESH)

    greet(sib)
    for t in range(1, chips):
        greet((d, peer(t)))
    for f in (2, 3):
        greet((there[f], e))
    for f in (0, 1):
        greet((there[f], 2 * (last - q) + c))
    pl.semaphore_wait(barrier, 1 + (chips - 1) + 2 + 2)

    lists_ref[pl.ds(q, 1)] = list_ref[...]
    for t in range(1, chips):
        pltpu.make_async_remote_copy(
            src_ref=list_ref,
            dst_ref=lists_ref.at[pl.ds(q, 1)],
            send_sem=list_sem.at[0, t],
            recv_sem=list_sem.at[1, t],
            device_id=(d, peer(t)),
            device_id_type=MESH,
        ).start()

    def list_copy(t):
        return pltpu.make_async_remote_copy(
            src_ref=list_ref,
            dst_ref=lists_ref.at[pl.ds((q + chips - t) % chips, 1)],
            send_sem=list_sem.at[0, t],
            recv_sem=list_sem.at[1, t],
            device_id=(d, peer(t)),
            device_id_type=MESH,
        )

    def exchange(l, own):
        def node_block(s, h, core=c):
            return (2 * s + core) * parts + h

        def halo_block(s, f, core=c):
            return count * parts + (2 * s + core) * FACES + f

        def block_at(block):
            return table_ref.at[l, rows(block * HALO, HALO), :]

        def copy(kind, block, who, src=None):
            return pltpu.make_async_remote_copy(
                src_ref=block_at(block) if src is None else src,
                dst_ref=block_at(block),
                send_sem=block_send.at[l, kind, block],
                recv_sem=block_recv.at[l, block],
                device_id=who,
                device_id_type=MESH,
            )

        sent = []

        def start(cond, kind, block, who, src=None):
            if cond is None:
                copy(kind, block, who, src).start()
            else:

                @pl.when(cond)
                def _():
                    copy(kind, block, who, src).start()

            return (kind, block, who, src)

        def wait(block):
            copy(SIDE, block, sib).wait_recv()

        ids = lax.broadcasted_iota(jnp.int32, (size, HALO), 0)

        def pick(s, f):
            hit = jnp.where(ids == lists_ref[s, f : f + 1, :], 1.0, 0.0).astype(BF16)
            values = table_ref[l, rows((2 * s + c) * size, size), :]
            face_ref[l, s, f] = lax.dot_general(
                hit, values, (((0,), (0,)), ((), ())), preferred_element_type=F32
            ).astype(BF16)

        def available(s):
            for edge_q, across in ((0, 2 * last + c), (last, c)):

                @pl.when((q == edge_q) & (s + edge_q != last if edge_q == 0 else s != 0))
                def _():
                    for f in (0, 1):
                        pick(s, f)
                        copy(
                            ACROSS, halo_block(s, f), (there[f], across), face_ref.at[l, s, f]
                        ).start()

            for f in (2, 3):
                pick(s, f)
                copy(ACROSS, halo_block(s, f), (there[f], e), face_ref.at[l, s, f]).start()

        table_ref[l, rows(e * size, size), :] = own
        for h in range(parts):
            start(q < last, UP, node_block(q, h), ups)
            start(q > 0, DOWN, node_block(q, h), downs)
        for h in range(parts):
            start(None, SIDE, node_block(q, h), sib)
        available(q)

        def from_line(s, onward, kind, who):
            for h in range(parts):
                block = node_block(s, h)
                wait(block)
                start(onward, kind, block, who)
                start(None, SIDE, block, sib)
            if l == 0:
                list_wait(s)
            available(s)

        def list_wait(s):
            for t in range(1, chips):

                @pl.when((q + chips - s) % chips == t)
                def _():
                    list_copy(t).wait_recv()

        def from_x(s):
            for f in (2, 3):
                block = halo_block(s, f)
                wait(block)
                start(None, SIDE, block, sib)

        def from_z(s, onward, kind, who):
            for f in (0, 1):
                block = halo_block(s, f)
                wait(block)
                if onward:
                    start(None, kind, block, who)
                start(None, SIDE, block, sib)

        for k in range(1, chips + 1):
            for flow, (kind, who) in enumerate(((DOWN, downs), (UP, ups))):
                for a, reach in enumerate(REACH):
                    place = chips + a - k
                    if place not in reach:
                        continue
                    s = last - a if flow else a
                    at = last - place if flow else place
                    onward = place - 1 in reach

                    @pl.when(q == at)
                    def _():
                        from_z(s, onward, kind, who)

            if k < chips:

                @pl.when(q >= k)
                def _():
                    from_line(q - k, q < last, UP, ups)

                @pl.when(q + k <= last)
                def _():
                    from_line(q + k, q > 0, DOWN, downs)

            if k == 1:
                from_x(q)
            else:

                @pl.when(q >= k - 1)
                def _():
                    from_x(q - (k - 1))

                @pl.when(q + k - 1 <= last)
                def _():
                    from_x(q + k - 1)

        def finish_nodes():
            for s in range(chips):
                for h in range(parts):
                    wait(node_block(s, h, 1 - c))

        def finish_halo():
            for s in range(chips):
                for f in range(FACES):
                    wait(halo_block(s, f, 1 - c))

        def finish_sends():
            for s in range(chips):
                for h in range(parts):
                    block = node_block(s, h)
                    pl.when((q < last) & (s <= q))(lambda: copy(UP, block, ups).wait_send())
                    pl.when((q > 0) & (s >= q))(lambda: copy(DOWN, block, downs).wait_send())
                    copy(SIDE, block, sib).wait_send()
                for f in range(FACES):
                    block = halo_block(s, f)
                    copy(SIDE, block, sib).wait_send()
                    if f >= 2:
                        copy(ACROSS, block, sib, face_ref.at[l, s, f]).wait_send()
                    else:
                        cond = (q == 0) if s != last else None
                        if s != 0:
                            cond = (q == last) if cond is None else cond | (q == last)
                        pl.when(cond)(
                            lambda: copy(ACROSS, block, sib, face_ref.at[l, s, f]).wait_send()
                        )
                        if s < len(REACH):
                            for place in REACH[s]:
                                if place - 1 in REACH[s]:
                                    pl.when(q == place)(
                                        lambda: copy(DOWN, block, downs).wait_send()
                                    )
                        if last - s < len(REACH):
                            for place in REACH[last - s]:
                                if place - 1 in REACH[last - s]:
                                    pl.when(q == last - place)(
                                        lambda: copy(UP, block, ups).wait_send()
                                    )

        return finish_nodes, finish_halo, finish_sends

    def project(l, out_ref, part, first, stop, bias):
        for base in range(first, stop, STEP):
            val = dot(
                table_ref[l, base : base + STEP, :],
                ew1_ref[l, part * width : (part + 1) * width, :],
            )
            if bias is not None:
                val = val + bias
            out_ref[pl.ds(base, STEP), 0, :] = val[:, :half]
            out_ref[pl.ds(base, STEP), 1, :] = val[:, half:]

    def edge_phase(l, in_ref, out_ref):
        @pl.loop(0, edges // GROUP)
        def _(g):
            for u in range(GROUP):
                k = g * GROUP + u
                a = send_ref[k]
                b = recv_ref[k]
                at = pl.multiple_of(g * (2 * GROUP), 2 * GROUP) + 2 * u
                pre_ref[pl.ds(at, 2), :] = s_ref[a] + r_ref[b]

        live = live_ref[0, 0]

        @pl.loop(0, edges // CHUNK)
        def _(i):
            base = pl.multiple_of(i * CHUNK, CHUNK)
            old = in_ref[pl.ds(base, CHUNK), :]
            pre = dot(old, ew1_ref[l, :width, :])
            low = pre[:, :half] + pre_ref[pl.ds(2 * base, CHUNK, stride=2), :]
            high = pre[:, half:] + pre_ref[pl.ds(2 * base + 1, CHUNK, stride=2), :]
            hidden = jnp.maximum(jnp.concatenate([low, high], axis=1), 0.0).astype(BF16)
            message = layer_norm(dot(hidden, ew2_ref[l]), eg_ref[l : l + 1, :])
            slot = lax.broadcasted_iota(jnp.int32, (CHUNK, 1), 0) + base
            message = jnp.where(slot < live, message, 0.0)
            out_ref[pl.ds(base, CHUNK), :] = (old.astype(F32) + message).astype(BF16)
            msg_ref[pl.ds(base, CHUNK), :] = message.astype(BF16)

    def scatter(owner):
        depth = 512
        ids = lax.broadcasted_iota(jnp.int32, (size, depth), 0) + owner * size
        acc = jnp.zeros((size, width), F32)
        for j in range(0, edges, depth):
            hit = ids == recv_row_ref[:, j : j + depth]
            acc = acc + dot(jnp.where(hit, 1.0, 0.0).astype(BF16), msg_ref[j : j + depth, :])
        return acc

    def reduce_phase(l, own):
        def pair_copy(t):
            return pltpu.make_async_remote_copy(
                src_ref=part_ref.at[l, t],
                dst_ref=pair_ref.at[l, t],
                send_sem=pair_sem.at[l, 0, t],
                recv_sem=pair_sem.at[l, 1, t],
                device_id=sib,
                device_id_type=MESH,
            )

        def sum_copy(t):
            return pltpu.make_async_remote_copy(
                src_ref=sums_ref.at[l, t],
                dst_ref=got_ref.at[l, t],
                send_sem=sum_sem.at[l, 0, t],
                recv_sem=sum_sem.at[l, 1, t],
                device_id=(d, peer(t)),
                device_id_type=MESH,
            )

        order = (2, 3, 1, 0)
        for t in order:
            part_ref[l, t] = scatter(2 * ((q + t) % chips) + 1 - c).astype(BF16)
            pair_copy(t).start()
        mine = None
        for t in order:
            total = scatter(peer(t))
            pair_copy(t).wait_recv()
            total = total + pair_ref[l, t].astype(F32)
            if t:
                sums_ref[l, t] = total.astype(BF16)
                sum_copy(t).start()
            else:
                mine = total
        pre = dot(own, nw1_ref[l, :width, :]) + nb1_ref[l : l + 1, :]
        for t in order[:-1]:
            sum_copy(t).wait_recv()
            mine = mine + got_ref[l, t].astype(F32)
        pre = pre + dot(mine.astype(BF16), nw1_ref[l, width:, :])
        hidden = jnp.maximum(pre, 0.0).astype(BF16)
        update = layer_norm(dot(hidden, nw2_ref[l]), ng_ref[l : l + 1, :])
        new = (own.astype(F32) + update).astype(BF16)

        def finish_sends():
            for t in order:
                pair_copy(t).wait_send()
                if t:
                    sum_copy(t).wait_send()

        return new, finish_sends

    own = own_ref[...]
    pending = []
    for l in range(LAYERS):
        finish_nodes, finish_halo, finish_sends = exchange(l, own)
        pending.append(finish_sends)
        finish_nodes()
        project(l, s_ref, 1, 0, nodes, None)
        project(l, r_ref, 2, 0, nodes, eb1_ref[l : l + 1, :])
        finish_halo()
        project(l, s_ref, 1, nodes, table_ref.shape[1], None)
        edge_phase(l, edge_ref if l == 0 else mid_ref, edge_out_ref if l == LAYERS - 1 else mid_ref)
        own, finish_sums = reduce_phase(l, own)
        pending.append(finish_sums)
    node_out_ref[...] = own
    for finish in pending:
        finish()
    for t in range(1, chips):
        list_copy(t).wait_send()


def shards(
    node_lat,
    edge_lat,
    senders,
    receivers,
    live_edges,
    send_rows,
    edge_w1,
    edge_b1,
    edge_w2,
    edge_gain,
    node_w1,
    node_b1,
    node_w2,
    node_gain,
):
    vmem = pl.BlockSpec(memory_space=pltpu.VMEM)
    smem = pl.BlockSpec(memory_space=pltpu.SMEM)
    dma = pltpu.SemaphoreType.DMA
    size, width = node_lat.shape
    edges = edge_lat.shape[0]
    count = lax.axis_size("edge")
    chips = count // 2
    nodes = count * size
    table = count * (size + FACES * HALO)
    blocks = table // HALO
    half = width // 2
    sums = pltpu.VMEM((LAYERS, chips, size, width), BF16)
    return pl.pallas_call(
        kernel,
        out_shape=(
            jax.ShapeDtypeStruct(node_lat.shape, BF16),
            jax.ShapeDtypeStruct(edge_lat.shape, BF16),
        ),
        in_specs=[vmem, vmem, smem, smem, vmem, smem] + [vmem] * 9,
        out_specs=(vmem, vmem),
        scratch_shapes=[
            pltpu.VMEM((LAYERS, table, width), BF16),
            pltpu.VMEM((LAYERS, chips, FACES, HALO, width), BF16),
            pltpu.VMEM((chips, FACES, HALO), jnp.int32),
            pltpu.VMEM((edges, width), BF16),
            pltpu.VMEM((table, 2, half), F32),
            pltpu.VMEM((nodes, 2, half), F32),
            pltpu.VMEM((2 * edges, half), F32),
            pltpu.VMEM((edges, width), BF16),
            sums,
            sums,
            sums,
            sums,
            dma((LAYERS, 4, blocks)),
            dma((LAYERS, blocks)),
            dma((2, chips)),
            dma((LAYERS, 2, chips)),
            dma((LAYERS, 2, chips)),
        ],
        compiler_params=pltpu.CompilerParams(
            collective_id=0, has_side_effects=True, vmem_limit_bytes=56 * 2**20
        ),
        cost_estimate=pl.CostEstimate(
            flops=2 * 10**10, bytes_accessed=8 * 2**20, transcendentals=0
        ),
        name="graph_layers",
    )(
        node_lat,
        edge_lat,
        senders,
        receivers,
        receivers.reshape(1, -1),
        live_edges,
        send_rows,
        edge_w1,
        edge_b1,
        edge_w2,
        edge_gain,
        node_w1,
        node_b1,
        node_w2,
        node_gain,
    )


def solution(mesh):
    split = P(("dom", "edge"), None)
    in_specs = (
        split,
        split,
        P(("dom", "edge")),
        P(("dom", "edge")),
        P("dom", "edge"),
        P(("dom", "edge"), None, None),
    ) + (P(),) * 8
    return jax.shard_map(
        shards, mesh=mesh, in_specs=in_specs, out_specs=(split, split), check_vma=False
    )
```

time: 488 us -> 129 us (0.26)
  waiting for transfers between devices: 231 us -> 0 us
  Pallas kernels: 0 us -> 123 us
  local copies, waits for them, and re-layouts: 103 us -> 4.22 us
  other arithmetic: 66.4 us -> 0 us
  matrix products: 29.4 us -> 0 us
  starting transfers between devices: 24.7 us -> 0 us
  blocking collectives: 15.9 us -> 0 us
  between operations: 14.8 us -> 1.29 us
    psum x2 -> x0, waiting for transfers between devices: 131 us -> none  [shards(): lax.psum(domain_sum.astype(jnp.bfloat16), 'edge').astype(jnp.float32)]
    pallas_call x0 -> x1, Pallas kernels: none -> 123 us  [shards(): pl.pallas_call(kernel, out_shape=(jax.ShapeDtypeStruct(node_lat.shape, BF...]
    gather x6 -> x0, local copies, waits for them, and re-layouts: 86.2 us -> none  [the longest x2 30.9 us: shards(): face_rows = jnp.take(domain_rows, lists_all, axis=0)]
    all_gather x2 -> x0, waiting for transfers between devices: 54.2 us -> none  [shards(): domain_rows = lax.all_gather(owned_rows, 'edge', axis=0, tiled=True)]
    ppermute x8 -> x0, waiting for transfers between devices: 45 us -> none  [passed_along(): return lax.ppermute(value, axis, pairs)]
    scatter-add x2 -> x0, other arithmetic: 38.6 us -> none  [shards(): jax.ops.segment_sum(messages, receivers, num_segments=node_count * rank_c...]
    dot_general x10 -> x0, matrix products: 29.4 us -> none  [the longest x2 10.6 us: edge_update(): jnp.dot(hidden_rows, weight_out, preferred_element_type=jnp.float32)]
    ppermute x8 -> x0, starting transfers between devices: 24.5 us -> none  [passed_along(): return lax.ppermute(value, axis, pairs)]
  transfers between devices with their start and end apart: 12 -> 0, of which waited for: 8 -> 0; matrix products, arithmetic and copies ran while one was open for 10% -> 0% of each run, Pallas kernels for 0% -> 0%
where the time goes in v2:
time: 129 us
  Pallas kernels  123 us (95%)
  local copies, waits for them, and re-layouts  4.22 us (3%)
  between operations  1.29 us (1%)
    pallas_call x1, Pallas kernels, shards(): pl.pallas_call(kernel, out_shape=(jax.ShapeDtypeStruct(node_lat.shape, BF...  123 us
    unnamed x2, local copies, waits for them, and re-layouts  4.22 us

profile of v2, /device:TPU:1, one launch (start us, length us, event | category | flops | bytes accessed | tf_op | source)
XLA Modules:
  0.0 128.6 jit_solution(10255889956072535248)
XLA Ops:
  1.3 123.1 %graph_layers.1 = (bf16[256,256]{1,0:T(8,128)(2,1)}, bf16[3072,256]{1,0:T(8,128)(2,1)}) custom-call(bf16[256,256]{1,0:T(8,128)(2,1)} %own_ref.1, bf16[3072,256]{1,0:T(8,128)(2,1)} %edge_ref.1, s32[3072]{0:T(1024)} %send_ref.1, s32[3072]{0:T(1024)} %recv_ref.1, s32[1,3072]{1,0:T(1,128)} %bitcast.1, s32[1,1]{1,0:T(1,128)S(6)} %copy.18.live_ref, ...), custom_call_target="tpu_custom_call" | custom-call | flops 20000000000 | bytes 8388608 | tf_op jit(solution)/shard_map/graph_layers/pallas_call | solution.py:454
  124.4 1.6 %copy.19 = bf16[256,256]{1,0:T(8,128)(2,1)} copy(bf16[256,256]{1,0:T(8,128)(2,1)} %get-tuple-element.4) | data formatting | bytes 262144
  126.0 2.7 %copy.20 = bf16[3072,256]{1,0:T(8,128)(2,1)} copy(bf16[3072,256]{1,0:T(8,128)(2,1)} %get-tuple-element.5) | data formatting | bytes 3145728

commit v3 on v2

v3 whole, which is shorter than its diff:
```python
import jax
import jax.numpy as jnp
from jax import lax
from jax.experimental import pallas as pl
from jax.experimental.pallas import tpu as pltpu
from jax.sharding import PartitionSpec as P

LAYERS = 2
EPS = 1e-05
FACES = 4
HALO = 128
GROUP = 32
CHUNK = 1024
STEP = 1024
MESH = pl.DeviceIdType.MESH
BF16 = jnp.bfloat16
F32 = jnp.float32
UP, DOWN, SIDE, ACROSS = range(4)
REACH = (0, 1, 3)


def dot(a, b):
    return jnp.dot(a, b, preferred_element_type=F32)


def layer_norm(values, gain):
    center = values - jnp.mean(values, axis=-1, keepdims=True)
    spread = jnp.mean(center * center, axis=-1, keepdims=True)
    return center * lax.rsqrt(spread + EPS) * gain


def rows(start, size):
    return pl.ds(pl.multiple_of(start, size), size)


def kernel(
    own_ref,
    edge_ref,
    send_ref,
    recv_ref,
    recv_row_ref,
    live_ref,
    list_ref,
    ew1_ref,
    eb1_ref,
    ew2_ref,
    eg_ref,
    nw1_ref,
    nb1_ref,
    nw2_ref,
    ng_ref,
    node_out_ref,
    edge_out_ref,
    table_ref,
    face_ref,
    lists_ref,
    mid_ref,
    s_ref,
    r_ref,
    pre_ref,
    msg_ref,
    part_ref,
    pair_ref,
    sums_ref,
    got_ref,
    sum_ref,
    node_ref,
    block_send,
    block_recv,
    list_sem,
    pair_sem,
    sum_sem,
    local_sem,
):
    d = lax.axis_index("dom")
    e = lax.axis_index("edge")
    doms = lax.axis_size("dom")
    count = lax.axis_size("edge")
    chips = count // 2
    last = chips - 1
    stride = doms // 4
    size, width = own_ref.shape
    half = width // 2
    edges = edge_ref.shape[0]
    nodes = count * size
    parts = size // HALO
    q = e // 2
    c = e % 2
    sib = (d, 2 * q + 1 - c)
    ups = (d, e + 2)
    downs = (d, e - 2)
    there = [(d + s) % doms for s in (1, doms - 1, stride, doms - stride)]

    def peer(t):
        return 2 * ((q + t) % chips) + c

    barrier = pltpu.get_barrier_semaphore()

    def greet(who):
        pl.semaphore_signal(barrier, inc=1, device_id=who, device_id_type=MESH)

    greet(sib)
    for t in range(1, chips):
        greet((d, peer(t)))
    for f in (2, 3):
        greet((there[f], e))
    for f in (0, 1):
        greet((there[f], 2 * (last - q) + c))
    pl.semaphore_wait(barrier, 1 + (chips - 1) + 2 + 2)

    def edge_load():
        return pltpu.make_async_copy(edge_ref, mid_ref, local_sem.at[0])

    def edge_store():
        return pltpu.make_async_copy(mid_ref, edge_out_ref, local_sem.at[1])

    def list_copy(t):
        return pltpu.make_async_remote_copy(
            src_ref=list_ref,
            dst_ref=lists_ref.at[pl.ds(q, 1)],
            send_sem=list_sem.at[0, t],
            recv_sem=list_sem.at[1, t],
            device_id=(d, peer(t)),
            device_id_type=MESH,
        )

    edge_load().start()
    lists_ref[pl.ds(q, 1)] = list_ref[...]
    for t in range(1, chips):
        list_copy(t).start()
    node_ref[...] = own_ref[...]

    def exchange(l):
        def node_block(s, h, core=c):
            return (2 * s + core) * parts + h

        def halo_block(s, f, core=c):
            return count * parts + (2 * s + core) * FACES + f

        def block_at(block):
            return table_ref.at[l, rows(block * HALO, HALO), :]

        def copy(kind, block, who, src=None):
            return pltpu.make_async_remote_copy(
                src_ref=block_at(block) if src is None else src,
                dst_ref=block_at(block),
                send_sem=block_send.at[l, kind, block],
                recv_sem=block_recv.at[l, block],
                device_id=who,
                device_id_type=MESH,
            )

        def start(cond, kind, block, who):
            if cond is None:
                copy(kind, block, who).start()
            else:
                pl.when(cond)(lambda: copy(kind, block, who).start())

        def wait(block):
            copy(SIDE, block, sib).wait_recv()

        ids = lax.broadcasted_iota(jnp.int32, (size, HALO), 0)

        def pick(s, f, who):
            hit = jnp.where(ids == lists_ref[s, pl.ds(f, 1), :], 1.0, 0.0).astype(BF16)
            values = table_ref[l, rows((2 * s + c) * size, size), :]
            face_ref[l, s, f] = lax.dot_general(
                hit, values, (((0,), (0,)), ((), ())), preferred_element_type=F32
            ).astype(BF16)
            copy(ACROSS, halo_block(s, f), who, face_ref.at[l, s, f]).start()

        def at_end(s):
            return ((q == 0) & (s != last)) | ((q == last) & (s != 0))

        def available(s):
            @pl.when(at_end(s))
            def _():
                @pl.loop(0, 2)
                def _(f):
                    pick(s, f, ((d + doms + 1 - 2 * f) % doms, 2 * (last - q) + c))

            @pl.loop(2, FACES)
            def _(f):
                pick(s, f, ((d + doms + stride * (5 - 2 * f)) % doms, e))

        table_ref[l, rows(e * size, size), :] = node_ref[...]
        for h in range(parts):
            start(q < last, UP, node_block(q, h), ups)
            start(q > 0, DOWN, node_block(q, h), downs)
        for h in range(parts):
            start(None, SIDE, node_block(q, h), sib)
        available(q)

        def from_line(s, onward, kind, who):
            for h in range(parts):
                block = node_block(s, h)
                wait(block)
                start(onward, kind, block, who)
                start(None, SIDE, block, sib)

            @pl.when(l == 0)
            def _():
                list_copy((q + chips - s) % chips).wait_recv()

            available(s)

        def from_x(s):
            for f in (2, 3):
                block = halo_block(s, f)
                wait(block)
                start(None, SIDE, block, sib)

        def from_z(s, onward, kind, who):
            for f in (0, 1):
                block = halo_block(s, f)
                wait(block)
                start(onward, kind, block, who)
                start(None, SIDE, block, sib)

        @pl.loop(1, chips + 1)
        def _(k):
            for kind, who in ((DOWN, downs), (UP, ups)):
                for a, least in enumerate(REACH):
                    place = chips + a - k
                    mine = q if kind == DOWN else last - q
                    s = a if kind == DOWN else last - a

                    @pl.when((mine == place) & (place >= least))
                    def _():
                        from_z(s, place > least, kind, who)

            @pl.when((k < chips) & (q >= k))
            def _():
                from_line(q - k, q < last, UP, ups)

            @pl.when((k < chips) & (q + k <= last))
            def _():
                from_line(q + k, q > 0, DOWN, downs)

            @pl.when(q >= k - 1)
            def _():
                from_x(q - (k - 1))

            @pl.when((k > 1) & (q + k - 1 <= last))
            def _():
                from_x(q + k - 1)

        def finish_nodes():
            @pl.loop(0, chips)
            def _(s):
                for h in range(parts):
                    wait(node_block(s, h, 1 - c))

        def finish_halo():
            @pl.loop(0, chips)
            def _(s):
                for f in range(FACES):
                    wait(halo_block(s, f, 1 - c))

        def finish_sends():
            for s in range(chips):
                low = REACH[s] if s < last else chips
                high = REACH[last - s] if s else chips
                for h in range(parts):
                    block = node_block(s, h)
                    pl.when((q < last) & (s <= q))(lambda: copy(UP, block, ups).wait_send())
                    pl.when((q > 0) & (s >= q))(lambda: copy(DOWN, block, downs).wait_send())
                    copy(SIDE, block, sib).wait_send()
                for f in range(FACES):
                    block = halo_block(s, f)
                    across = copy(ACROSS, block, sib, face_ref.at[l, s, f])
                    copy(SIDE, block, sib).wait_send()
                    if f >= 2:
                        across.wait_send()
                    else:
                        pl.when(at_end(s))(across.wait_send)
                        pl.when(q > low)(lambda: copy(DOWN, block, downs).wait_send())
                        pl.when(last - q > high)(lambda: copy(UP, block, ups).wait_send())

        return finish_nodes, finish_halo, finish_sends

    def project(l, out_ref, part, first, stop, bias):
        @pl.loop(first // STEP, stop // STEP)
        def _(i):
            base = pl.multiple_of(i * STEP, STEP)
            val = dot(
                table_ref[l, pl.ds(base, STEP), :],
                ew1_ref[l, part * width : (part + 1) * width, :],
            )
            if bias is not None:
                val = val + bias
            out_ref[pl.ds(2 * base, STEP, stride=2), :] = val[:, :half]
            out_ref[pl.ds(2 * base + 1, STEP, stride=2), :] = val[:, half:]

    def edge_phase(l):
        @pl.loop(0, edges // GROUP)
        def _(g):
            for u in range(GROUP):
                k = g * GROUP + u
                a = send_ref[k]
                b = recv_ref[k]
                at = pl.multiple_of(g * (2 * GROUP), 2 * GROUP) + 2 * u
                pre_ref[pl.ds(at, 2), :] = s_ref[pl.ds(2 * a, 2), :] + r_ref[pl.ds(2 * b, 2), :]

        pl.when(l == 0)(lambda: edge_load().wait())
        live = live_ref[0, 0]

        @pl.loop(0, edges // CHUNK)
        def _(i):
            base = pl.multiple_of(i * CHUNK, CHUNK)
            old = mid_ref[pl.ds(base, CHUNK), :]
            pre = dot(old, ew1_ref[l, :width, :])
            low = pre[:, :half] + pre_ref[pl.ds(2 * base, CHUNK, stride=2), :]
            high = pre[:, half:] + pre_ref[pl.ds(2 * base + 1, CHUNK, stride=2), :]
            hidden = jnp.maximum(jnp.concatenate([low, high], axis=1), 0.0).astype(BF16)
            message = layer_norm(dot(hidden, ew2_ref[l]), eg_ref[pl.ds(l, 1), :])
            slot = lax.broadcasted_iota(jnp.int32, (CHUNK, 1), 0) + base
            message = jnp.where(slot < live, message, 0.0)
            mid_ref[pl.ds(base, CHUNK), :] = (old.astype(F32) + message).astype(BF16)
            msg_ref[pl.ds(base, CHUNK), :] = message.astype(BF16)

        pl.when(l == LAYERS - 1)(lambda: edge_store().start())

    def scatter(owner):
        depth = 512
        ids = lax.broadcasted_iota(jnp.int32, (size, depth), 0) + owner * size
        acc = jnp.zeros((size, width), F32)
        for j in range(0, edges, depth):
            hit = ids == recv_row_ref[:, j : j + depth]
            acc = acc + dot(jnp.where(hit, 1.0, 0.0).astype(BF16), msg_ref[j : j + depth, :])
        return acc

    def reduce_phase(l):
        def pair_copy(t):
            return pltpu.make_async_remote_copy(
                src_ref=part_ref.at[l, t],
                dst_ref=pair_ref.at[l, t],
                send_sem=pair_sem.at[l, 0, t],
                recv_sem=pair_sem.at[l, 1, t],
                device_id=sib,
                device_id_type=MESH,
            )

        def sum_copy(t):
            return pltpu.make_async_remote_copy(
                src_ref=sums_ref.at[l, t],
                dst_ref=got_ref.at[l, t],
                send_sem=sum_sem.at[l, 0, t],
                recv_sem=sum_sem.at[l, 1, t],
                device_id=(d, peer(t)),
                device_id_type=MESH,
            )

        @pl.loop(1, chips + 1)
        def _(i):
            t = i % chips
            part_ref[l, t] = scatter(2 * ((q + t) % chips) + 1 - c).astype(BF16)
            pair_copy(t).start()

        @pl.loop(1, chips + 1)
        def _(i):
            t = i % chips
            total = scatter(peer(t))
            pair_copy(t).wait_recv()
            total = total + pair_ref[l, t].astype(F32)
            sum_ref[...] = total
            sums_ref[l, t] = total.astype(BF16)
            pl.when(t > 0)(lambda: sum_copy(t).start())

        own = node_ref[...]
        mine = sum_ref[...]
        pre = dot(own, nw1_ref[l, :width, :]) + nb1_ref[pl.ds(l, 1), :]
        for t in range(1, chips):
            sum_copy(t).wait_recv()
            mine = mine + got_ref[l, t].astype(F32)
        pre = pre + dot(mine.astype(BF16), nw1_ref[l, width:, :])
        hidden = jnp.maximum(pre, 0.0).astype(BF16)
        update = layer_norm(dot(hidden, nw2_ref[l]), ng_ref[pl.ds(l, 1), :])
        node_ref[...] = (own.astype(F32) + update).astype(BF16)
        for t in range(chips):
            pair_copy(t).wait_send()
            if t:
                sum_copy(t).wait_send()

    @pl.loop(0, LAYERS)
    def _(l):
        finish_nodes, finish_halo, finish_sends = exchange(l)
        finish_nodes()
        project(l, s_ref, 1, 0, nodes, None)
        project(l, r_ref, 2, 0, nodes, eb1_ref[pl.ds(l, 1), :])
        finish_halo()
        project(l, s_ref, 1, nodes, table_ref.shape[1], None)
        edge_phase(l)
        finish_sends()
        reduce_phase(l)

    node_out_ref[...] = node_ref[...]
    edge_store().wait()
    for t in range(1, chips):
        list_copy(t).wait_send()


def settle_kernel(node_ref, edge_ref, node_out_ref, edge_out_ref, node_buf, edge_buf, sems):
    pieces = 4
    size = edge_ref.shape[0] // pieces
    moves = [(node_ref, node_buf, node_out_ref)]
    for i in range(pieces):
        part = pl.ds(i * size, size)
        moves.append((edge_ref.at[part], edge_buf.at[part], edge_out_ref.at[part]))
    loads = [
        pltpu.make_async_copy(move[0], move[1], sems.at[0, i]) for i, move in enumerate(moves)
    ]
    stores = [
        pltpu.make_async_copy(move[1], move[2], sems.at[1, i]) for i, move in enumerate(moves)
    ]
    for load in loads:
        load.start()
    for load, store in zip(loads, stores):
        load.wait()
        store.start()
    for store in stores:
        store.wait()


def shards(
    node_lat,
    edge_lat,
    senders,
    receivers,
    live_edges,
    send_rows,
    edge_w1,
    edge_b1,
    edge_w2,
    edge_gain,
    node_w1,
    node_b1,
    node_w2,
    node_gain,
):
    vmem = pl.BlockSpec(memory_space=pltpu.VMEM)
    smem = pl.BlockSpec(memory_space=pltpu.SMEM)
    hbm = pl.BlockSpec(memory_space=pl.ANY)
    dma = pltpu.SemaphoreType.DMA
    size, width = node_lat.shape
    edges = edge_lat.shape[0]
    count = lax.axis_size("edge")
    chips = count // 2
    nodes = count * size
    table = count * (size + FACES * HALO)
    blocks = table // HALO
    half = width // 2
    sums = pltpu.VMEM((LAYERS, chips, size, width), BF16)
    outs = (
        jax.ShapeDtypeStruct(node_lat.shape, BF16),
        jax.ShapeDtypeStruct(edge_lat.shape, BF16),
    )
    own, moved = pl.pallas_call(
        kernel,
        out_shape=outs,
        in_specs=[vmem, hbm, smem, smem, vmem, smem] + [vmem] * 9,
        out_specs=(vmem, hbm),
        scratch_shapes=[
            pltpu.VMEM((LAYERS, table, width), BF16),
            pltpu.VMEM((LAYERS, chips, FACES, HALO, width), BF16),
            pltpu.VMEM((chips, FACES, HALO), jnp.int32),
            pltpu.VMEM((edges, width), BF16),
            pltpu.VMEM((2 * table, half), F32),
            pltpu.VMEM((2 * nodes, half), F32),
            pltpu.VMEM((2 * edges, half), F32),
            pltpu.VMEM((edges, width), BF16),
            sums,
            sums,
            sums,
            sums,
            pltpu.VMEM((size, width), F32),
            pltpu.VMEM((size, width), BF16),
            dma((LAYERS, 4, blocks)),
            dma((LAYERS, blocks)),
            dma((2, chips)),
            dma((LAYERS, 2, chips)),
            dma((LAYERS, 2, chips)),
            dma((2,)),
        ],
        compiler_params=pltpu.CompilerParams(
            collective_id=0, has_side_effects=True, vmem_limit_bytes=56 * 2**20
        ),
        cost_estimate=pl.CostEstimate(
            flops=2 * 10**10, bytes_accessed=8 * 2**20, transcendentals=0
        ),
        name="graph_layers",
    )(
        node_lat,
        edge_lat,
        senders,
        receivers,
        receivers.reshape(1, -1),
        live_edges,
        send_rows,
        edge_w1,
        edge_b1,
        edge_w2,
        edge_gain,
        node_w1,
        node_b1,
        node_w2,
        node_gain,
    )
    return pl.pallas_call(
        settle_kernel,
        out_shape=outs,
        in_specs=[hbm, hbm],
        out_specs=(hbm, hbm),
        scratch_shapes=[
            pltpu.VMEM(node_lat.shape, BF16),
            pltpu.VMEM(edge_lat.shape, BF16),
            dma((2, 5)),
        ],
        name="settle",
    )(own, moved)


def solution(mesh):
    split = P(("dom", "edge"), None)
    in_specs = (
        split,
        split,
        P(("dom", "edge")),
        P(("dom", "edge")),
        P("dom", "edge"),
        P(("dom", "edge"), None, None),
    ) + (P(),) * 8
    return jax.shard_map(
        shards, mesh=mesh, in_specs=in_specs, out_specs=(split, split), check_vma=False
    )
```

time: 129 us -> 118 us (0.915)
  Pallas kernels: 123 us -> 116 us
  local copies, waits for them, and re-layouts: 4.22 us -> 0 us
    pallas_call x1 -> x2, Pallas kernels: 123 us -> 116 us  [the longest x1 114 us: shards(): pl.pallas_call(kernel, out_shape=outs, in_specs=[vmem, hbm, smem, smem, v...]
    unnamed x2 -> x0, local copies, waits for them, and re-layouts: 4.22 us -> none
where the time goes in v3:
time: 118 us
  Pallas kernels  116 us (98%)
  between operations  1.29 us (1%)
    pallas_call x1, Pallas kernels, shards(): pl.pallas_call(kernel, out_shape=outs, in_specs=[vmem, hbm, smem, smem, v...  114 us

profile of v3, /device:TPU:1, one launch (start us, length us, event | category | flops | bytes accessed | tf_op | source)
XLA Modules:
  0.0 117.6 jit_solution(1260586153312421070)
XLA Ops:
  1.3 114.0 %graph_layers.1 = (bf16[256,256]{1,0:T(8,128)(2,1)}, bf16[3072,256]{1,0:T(8,128)(2,1)}) custom-call(bf16[256,256]{1,0:T(8,128)(2,1)} %own_ref.1, bf16[3072,256]{1,0:T(8,128)(2,1)} %edge_ref.1, s32[3072]{0:T(1024)} %send_ref.1, s32[3072]{0:T(1024)} %recv_ref.1, s32[1,3072]{1,0:T(1,128)} %bitcast.1, s32[1,1]{1,0:T(1,128)S(6)} %copy.16.live_ref, ...), custom_call_target="tpu_custom_call" | custom-call | flops 20000000000 | bytes 8388608 | tf_op jit(solution)/shard_map/graph_layers/pallas_call | solution.py:458
  115.3 2.3 %settle.1 = (bf16[256,256]{1,0:T(8,128)(2,1)}, bf16[3072,256]{1,0:T(8,128)(2,1)}) custom-call(bf16[256,256]{1,0:T(8,128)(2,1)} %get-tuple-element.4.node_ref, bf16[3072,256]{1,0:T(8,128)(2,1)} %get-tuple-element.5.edge_ref), custom_call_target="tpu_custom_call" | custom-call | tf_op jit(solution)/shard_map/settle/pallas_call | solution.py:509

commit v4 on v3

--- a/solution.py
+++ b/solution.py
@@ -15,7 +15,7 @@
 MESH = pl.DeviceIdType.MESH
 BF16 = jnp.bfloat16
 F32 = jnp.float32
-UP, DOWN, SIDE, ACROSS = range(4)
+UP, DOWN, SIDE, ACROSS, BEYOND = range(5)
 REACH = (0, 1, 3)
 
 
@@ -38,9 +38,20 @@
     edge_ref,
     send_ref,
     recv_ref,
-    recv_row_ref,
     live_ref,
     list_ref,
+    recv_row_hbm,
+    ew1_hbm,
+    eb1_hbm,
+    ew2_hbm,
+    eg_hbm,
+    nw1_hbm,
+    nb1_hbm,
+    nw2_hbm,
+    ng_hbm,
+    node_out_ref,
+    edge_out_ref,
+    recv_row_ref,
     ew1_ref,
     eb1_ref,
     ew2_ref,
@@ -49,8 +60,6 @@
     nb1_ref,
     nw2_ref,
     ng_ref,
-    node_out_ref,
-    edge_out_ref,
     table_ref,
     face_ref,
     lists_ref,
@@ -71,6 +80,7 @@
     pair_sem,
     sum_sem,
     local_sem,
+    load_sem,
 ):
     d = lax.axis_index("dom")
     e = lax.axis_index("edge")
@@ -87,12 +97,36 @@
     q = e // 2
     c = e % 2
     sib = (d, 2 * q + 1 - c)
+    beside = q + 1 - 2 * (q % 2)
     ups = (d, e + 2)
     downs = (d, e - 2)
     there = [(d + s) % doms for s in (1, doms - 1, stride, doms - stride)]
 
     def peer(t):
         return 2 * ((q + t) % chips) + c
+
+    def loads():
+        pairs = (
+            (ew1_hbm, ew1_ref),
+            (eb1_hbm, eb1_ref),
+            (ew2_hbm, ew2_ref),
+            (eg_hbm, eg_ref),
+            (recv_row_hbm, recv_row_ref),
+            (nw1_hbm, nw1_ref),
+            (nb1_hbm, nb1_ref),
+            (nw2_hbm, nw2_ref),
+            (ng_hbm, ng_ref),
+        )
+        return [
+            pltpu.make_async_copy(src, dst, load_sem.at[i]) for i, (src, dst) in enumerate(pairs)
+        ]
+
+    def edge_load():
+        return pltpu.make_async_copy(edge_ref, mid_ref, local_sem.at[0])
+
+    for load in loads():
+        load.start()
+    edge_load().start()
 
     barrier = pltpu.get_barrier_semaphore()
 
@@ -106,10 +140,8 @@
         greet((there[f], e))
     for f in (0, 1):
         greet((there[f], 2 * (last - q) + c))
-    pl.semaphore_wait(barrier, 1 + (chips - 1) + 2 + 2)
-
-    def edge_load():
-        return pltpu.make_async_copy(edge_ref, mid_ref, local_sem.at[0])
+        greet((there[f], 2 * beside + c))
+    pl.semaphore_wait(barrier, 1 + (chips - 1) + 2 + 2 + 2)
 
     def edge_store():
         return pltpu.make_async_copy(mid_ref, edge_out_ref, local_sem.at[1])
@@ -124,7 +156,6 @@
             device_id_type=MESH,
         )
 
-    edge_load().start()
     lists_ref[pl.ds(q, 1)] = list_ref[...]
     for t in range(1, chips):
         list_copy(t).start()
@@ -172,12 +203,22 @@
         def at_end(s):
             return ((q == 0) & (s != last)) | ((q == last) & (s != 0))
 
+        def twice(s):
+            return ((q == 0) & (s < last - 1)) | ((q == last) & (s > 1))
+
         def available(s):
             @pl.when(at_end(s))
             def _():
                 @pl.loop(0, 2)
                 def _(f):
-                    pick(s, f, ((d + doms + 1 - 2 * f) % doms, 2 * (last - q) + c))
+                    dom = (d + doms + 1 - 2 * f) % doms
+                    pick(s, f, (dom, 2 * (last - q) + c))
+
+                    @pl.when(twice(s))
+                    def _():
+                        copy(
+                            BEYOND, halo_block(s, f), (dom, 2 * beside + c), face_ref.at[l, s, f]
+                        ).start()
 
             @pl.loop(2, FACES)
             def _(f):
@@ -221,13 +262,13 @@
         def _(k):
             for kind, who in ((DOWN, downs), (UP, ups)):
                 for a, least in enumerate(REACH):
-                    place = chips + a - k
                     mine = q if kind == DOWN else last - q
                     s = a if kind == DOWN else last - a
-
-                    @pl.when((mine == place) & (place >= least))
+                    entry = mine % 2 == 1
+
+                    @pl.when((k == 2 + a - mine % 2) & (mine >= least))
                     def _():
-                        from_z(s, place > least, kind, who)
+                        from_z(s, entry & (mine > least), kind, who)
 
             @pl.when((k < chips) & (q >= k))
             def _():
@@ -274,8 +315,10 @@
                         across.wait_send()
                     else:
                         pl.when(at_end(s))(across.wait_send)
-                        pl.when(q > low)(lambda: copy(DOWN, block, downs).wait_send())
-                        pl.when(last - q > high)(lambda: copy(UP, block, ups).wait_send())
+                        beyond = copy(BEYOND, block, sib, face_ref.at[l, s, f])
+                        pl.when(twice(s))(beyond.wait_send)
+                        pl.when((q > low) & (q % 2 == 1))(lambda: copy(DOWN, block, downs).wait_send())
+                        pl.when((last - q > high) & (q % 2 == 0))(lambda: copy(UP, block, ups).wait_send())
 
         return finish_nodes, finish_halo, finish_sends
 
@@ -330,7 +373,7 @@
             acc = acc + dot(jnp.where(hit, 1.0, 0.0).astype(BF16), msg_ref[j : j + depth, :])
         return acc
 
-    def reduce_phase(l):
+    def reduce_phase(l, finish_sends):
         def pair_copy(t):
             return pltpu.make_async_remote_copy(
                 src_ref=part_ref.at[l, t],
@@ -351,15 +394,14 @@
                 device_id_type=MESH,
             )
 
-        @pl.loop(1, chips + 1)
-        def _(i):
-            t = i % chips
+        def turn(i):
+            return (1 - i // 2) * (2 - i) + (i // 2) * (9 - 3 * i)
+
+        def give(t):
             part_ref[l, t] = scatter(2 * ((q + t) % chips) + 1 - c).astype(BF16)
             pair_copy(t).start()
 
-        @pl.loop(1, chips + 1)
-        def _(i):
-            t = i % chips
+        def gain(t):
             total = scatter(peer(t))
             pair_copy(t).wait_recv()
             total = total + pair_ref[l, t].astype(F32)
@@ -367,6 +409,15 @@
             sums_ref[l, t] = total.astype(BF16)
             pl.when(t > 0)(lambda: sum_copy(t).start())
 
+        give(2)
+
+        @pl.loop(1, chips)
+        def _(i):
+            give(turn(i))
+            gain(turn(i - 1))
+
+        gain(0)
+        finish_sends()
         own = node_ref[...]
         mine = sum_ref[...]
         pre = dot(own, nw1_ref[l, :width, :]) + nb1_ref[pl.ds(l, 1), :]
@@ -386,13 +437,18 @@
     def _(l):
         finish_nodes, finish_halo, finish_sends = exchange(l)
         finish_nodes()
+
+        @pl.when(l == 0)
+        def _():
+            for load in loads():
+                load.wait()
+
         project(l, s_ref, 1, 0, nodes, None)
         project(l, r_ref, 2, 0, nodes, eb1_ref[pl.ds(l, 1), :])
         finish_halo()
         project(l, s_ref, 1, nodes, table_ref.shape[1], None)
         edge_phase(l)
-        finish_sends()
-        reduce_phase(l)
+        reduce_phase(l, finish_sends)
 
     node_out_ref[...] = node_ref[...]
     edge_store().wait()
@@ -450,6 +506,7 @@
     table = count * (size + FACES * HALO)
     blocks = table // HALO
     half = width // 2
+    weights = (edge_w1, edge_b1, edge_w2, edge_gain, node_w1, node_b1, node_w2, node_gain)
     sums = pltpu.VMEM((LAYERS, chips, size, width), BF16)
     outs = (
         jax.ShapeDtypeStruct(node_lat.shape, BF16),
@@ -458,9 +515,11 @@
     own, moved = pl.pallas_call(
         kernel,
         out_shape=outs,
-        in_specs=[vmem, hbm, smem, smem, vmem, smem] + [vmem] * 9,
+        in_specs=[vmem, hbm, smem, smem, smem, vmem] + [hbm] * 9,
         out_specs=(vmem, hbm),
         scratch_shapes=[
+            pltpu.VMEM((1, edges), jnp.int32),
+            *(pltpu.VMEM(value.shape, value.dtype) for value in weights),
             pltpu.VMEM((LAYERS, table, width), BF16),
             pltpu.VMEM((LAYERS, chips, FACES, HALO, width), BF16),
             pltpu.VMEM((chips, FACES, HALO), jnp.int32),
@@ -475,12 +534,13 @@
             sums,
             pltpu.VMEM((size, width), F32),
             pltpu.VMEM((size, width), BF16),
-            dma((LAYERS, 4, blocks)),
+            dma((LAYERS, 5, blocks)),
             dma((LAYERS, blocks)),
             dma((2, chips)),
             dma((LAYERS, 2, chips)),
             dma((LAYERS, 2, chips)),
             dma((2,)),
+            dma((1 + len(weights),)),
         ],
         compiler_params=pltpu.CompilerParams(
             collective_id=0, has_side_effects=True, vmem_limit_bytes=56 * 2**20
@@ -494,9 +554,9 @@
         edge_lat,
         senders,
         receivers,
-        receivers.reshape(1, -1),
         live_edges,
         send_rows,
+        receivers.reshape(1, -1),
         edge_w1,
         edge_b1,
         edge_w2,

time: 118 us -> 125 us (1.059)
  Pallas kernels: 116 us -> 123 us
    pallas_call x1, Pallas kernels: 114 us -> 121 us  [shards(): pl.pallas_call(kernel, out_shape=outs, in_specs=[vmem, hbm, smem, smem, s...]
where the time goes in v4:
time: 125 us
  Pallas kernels  123 us (98%)
  between operations  1.29 us (1%)
    pallas_call x1, Pallas kernels, shards(): pl.pallas_call(kernel, out_shape=outs, in_specs=[vmem, hbm, smem, smem, s...  121 us

profile of v4, /device:TPU:1, one launch (start us, length us, event | category | flops | bytes accessed | tf_op | source)
XLA Modules:
  0.0 124.6 jit_solution(11505892219154186579)
XLA Ops:
  1.3 121.0 %graph_layers.1 = (bf16[256,256]{1,0:T(8,128)(2,1)}, bf16[3072,256]{1,0:T(8,128)(2,1)}) custom-call(bf16[256,256]{1,0:T(8,128)(2,1)} %own_ref.1, bf16[3072,256]{1,0:T(8,128)(2,1)} %edge_ref.1, s32[3072]{0:T(1024)} %send_ref.1, s32[3072]{0:T(1024)} %recv_ref.1, s32[1,1]{1,0:T(1,128)S(6)} %copy.16.live_ref, s32[1,4,128]{2,1,0:T(4,128)} %list_ref.1, ...), custom_call_target="tpu_custom_call" | custom-call | flops 20000000000 | bytes 8388608 | tf_op jit(solution)/shard_map/graph_layers/pallas_call | solution.py:515
  122.3 2.3 %settle.1 = (bf16[256,256]{1,0:T(8,128)(2,1)}, bf16[3072,256]{1,0:T(8,128)(2,1)}) custom-call(bf16[256,256]{1,0:T(8,128)(2,1)} %get-tuple-element.4.node_ref, bf16[3072,256]{1,0:T(8,128)(2,1)} %get-tuple-element.5.edge_ref), custom_call_target="tpu_custom_call" | custom-call | tf_op jit(solution)/shard_map/settle/pallas_call | solution.py:569

commit v5 on v4

--- a/solution.py
+++ b/solution.py
@@ -9,13 +9,13 @@
 EPS = 1e-05
 FACES = 4
 HALO = 128
-GROUP = 32
-CHUNK = 1024
+GROUP = 128
+CHUNK = 1536
 STEP = 1024
 MESH = pl.DeviceIdType.MESH
 BF16 = jnp.bfloat16
 F32 = jnp.float32
-UP, DOWN, SIDE, ACROSS, BEYOND = range(5)
+UP, DOWN, SIDE, ACROSS = range(4)
 REACH = (0, 1, 3)
 
 
@@ -97,7 +97,6 @@
     q = e // 2
     c = e % 2
     sib = (d, 2 * q + 1 - c)
-    beside = q + 1 - 2 * (q % 2)
     ups = (d, e + 2)
     downs = (d, e - 2)
     there = [(d + s) % doms for s in (1, doms - 1, stride, doms - stride)]
@@ -140,8 +139,7 @@
         greet((there[f], e))
     for f in (0, 1):
         greet((there[f], 2 * (last - q) + c))
-        greet((there[f], 2 * beside + c))
-    pl.semaphore_wait(barrier, 1 + (chips - 1) + 2 + 2 + 2)
+    pl.semaphore_wait(barrier, 1 + (chips - 1) + 2 + 2)
 
     def edge_store():
         return pltpu.make_async_copy(mid_ref, edge_out_ref, local_sem.at[1])
@@ -203,22 +201,12 @@
         def at_end(s):
             return ((q == 0) & (s != last)) | ((q == last) & (s != 0))
 
-        def twice(s):
-            return ((q == 0) & (s < last - 1)) | ((q == last) & (s > 1))
-
         def available(s):
             @pl.when(at_end(s))
             def _():
                 @pl.loop(0, 2)
                 def _(f):
-                    dom = (d + doms + 1 - 2 * f) % doms
-                    pick(s, f, (dom, 2 * (last - q) + c))
-
-                    @pl.when(twice(s))
-                    def _():
-                        copy(
-                            BEYOND, halo_block(s, f), (dom, 2 * beside + c), face_ref.at[l, s, f]
-                        ).start()
+                    pick(s, f, ((d + doms + 1 - 2 * f) % doms, 2 * (last - q) + c))
 
             @pl.loop(2, FACES)
             def _(f):
@@ -262,13 +250,13 @@
         def _(k):
             for kind, who in ((DOWN, downs), (UP, ups)):
                 for a, least in enumerate(REACH):
+                    place = chips + a - k
                     mine = q if kind == DOWN else last - q
                     s = a if kind == DOWN else last - a
-                    entry = mine % 2 == 1
-
-                    @pl.when((k == 2 + a - mine % 2) & (mine >= least))
+
+                    @pl.when((mine == place) & (place >= least))
                     def _():
-                        from_z(s, entry & (mine > least), kind, who)
+                        from_z(s, place > least, kind, who)
 
             @pl.when((k < chips) & (q >= k))
             def _():
@@ -315,10 +303,8 @@
                         across.wait_send()
                     else:
                         pl.when(at_end(s))(across.wait_send)
-                        beyond = copy(BEYOND, block, sib, face_ref.at[l, s, f])
-                        pl.when(twice(s))(beyond.wait_send)
-                        pl.when((q > low) & (q % 2 == 1))(lambda: copy(DOWN, block, downs).wait_send())
-                        pl.when((last - q > high) & (q % 2 == 0))(lambda: copy(UP, block, ups).wait_send())
+                        pl.when(q > low)(lambda: copy(DOWN, block, downs).wait_send())
+                        pl.when(last - q > high)(lambda: copy(UP, block, ups).wait_send())
 
         return finish_nodes, finish_halo, finish_sends
 
@@ -534,7 +520,7 @@
             sums,
             pltpu.VMEM((size, width), F32),
             pltpu.VMEM((size, width), BF16),
-            dma((LAYERS, 5, blocks)),
+            dma((LAYERS, 4, blocks)),
             dma((LAYERS, blocks)),
             dma((2, chips)),
             dma((LAYERS, 2, chips)),

time: 125 us -> 115 us (0.920)
  Pallas kernels: 123 us -> 114 us
    pallas_call x1, Pallas kernels: 121 us -> 112 us  [shards(): pl.pallas_call(kernel, out_shape=outs, in_specs=[vmem, hbm, smem, smem, s...]
where the time goes in v5:
time: 115 us
  Pallas kernels  114 us (99%)
  between operations  1.29 us (1%)
    pallas_call x1, Pallas kernels, shards(): pl.pallas_call(kernel, out_shape=outs, in_specs=[vmem, hbm, smem, smem, s...  112 us

profile of v5, /device:TPU:1, one launch (start us, length us, event | category | flops | bytes accessed | tf_op | source)
XLA Modules:
  0.0 115.1 jit_solution(12134230376033864388)
XLA Ops:
  1.3 111.5 %graph_layers.1 = (bf16[256,256]{1,0:T(8,128)(2,1)}, bf16[3072,256]{1,0:T(8,128)(2,1)}) custom-call(bf16[256,256]{1,0:T(8,128)(2,1)} %own_ref.1, bf16[3072,256]{1,0:T(8,128)(2,1)} %edge_ref.1, s32[3072]{0:T(1024)} %send_ref.1, s32[3072]{0:T(1024)} %recv_ref.1, s32[1,1]{1,0:T(1,128)S(6)} %copy.16.live_ref, s32[1,4,128]{2,1,0:T(4,128)} %list_ref.1, ...), custom_call_target="tpu_custom_call" | custom-call | flops 20000000000 | bytes 8388608 | tf_op jit(solution)/shard_map/graph_layers/pallas_call | solution.py:501
  112.8 2.3 %settle.1 = (bf16[256,256]{1,0:T(8,128)(2,1)}, bf16[3072,256]{1,0:T(8,128)(2,1)}) custom-call(bf16[256,256]{1,0:T(8,128)(2,1)} %get-tuple-element.4.node_ref, bf16[3072,256]{1,0:T(8,128)(2,1)} %get-tuple-element.5.edge_ref), custom_call_target="tpu_custom_call" | custom-call | tf_op jit(solution)/shard_map/settle/pallas_call | solution.py:555

commit v6 on v5

--- a/solution.py
+++ b/solution.py
@@ -248,6 +248,14 @@
 
         @pl.loop(1, chips + 1)
         def _(k):
+            @pl.when((k < chips) & (q >= k))
+            def _():
+                from_line(q - k, q < last, UP, ups)
+
+            @pl.when((k < chips) & (q + k <= last))
+            def _():
+                from_line(q + k, q > 0, DOWN, downs)
+
             for kind, who in ((DOWN, downs), (UP, ups)):
                 for a, least in enumerate(REACH):
                     place = chips + a - k
@@ -257,14 +265,6 @@
                     @pl.when((mine == place) & (place >= least))
                     def _():
                         from_z(s, place > least, kind, who)
-
-            @pl.when((k < chips) & (q >= k))
-            def _():
-                from_line(q - k, q < last, UP, ups)
-
-            @pl.when((k < chips) & (q + k <= last))
-            def _():
-                from_line(q + k, q > 0, DOWN, downs)
 
             @pl.when(q >= k - 1)
             def _():

time: 115 us -> 113 us (0.983)
  Pallas kernels: 114 us -> 111 us
    pallas_call x1, Pallas kernels: 112 us -> 109 us  [shards(): pl.pallas_call(kernel, out_shape=outs, in_specs=[vmem, hbm, smem, smem, s...]
where the time goes in v6:
time: 113 us; the launch traced here: 112 us
  Pallas kernels  111 us (98%)
  between operations  1.29 us (1%)
    pallas_call x1, Pallas kernels, shards(): pl.pallas_call(kernel, out_shape=outs, in_specs=[vmem, hbm, smem, smem, s...  109 us
    pallas_call x1, Pallas kernels, shards(): pl.pallas_call(settle_kernel, out_shape=outs, in_specs=[hbm, hbm], out_sp...  2.29 us

profile of v6, /device:TPU:1, one launch (start us, length us, event | category | flops | bytes accessed | tf_op | source)
XLA Modules:
  0.0 112.4 jit_solution(18086457218196973645)
XLA Ops:
  1.3 108.9 %graph_layers.1 = (bf16[256,256]{1,0:T(8,128)(2,1)}, bf16[3072,256]{1,0:T(8,128)(2,1)}) custom-call(bf16[256,256]{1,0:T(8,128)(2,1)} %own_ref.1, bf16[3072,256]{1,0:T(8,128)(2,1)} %edge_ref.1, s32[3072]{0:T(1024)} %send_ref.1, s32[3072]{0:T(1024)} %recv_ref.1, s32[1,1]{1,0:T(1,128)S(6)} %copy.16.live_ref, s32[1,4,128]{2,1,0:T(4,128)} %list_ref.1, ...), custom_call_target="tpu_custom_call" | custom-call | flops 20000000000 | bytes 8388608 | tf_op jit(solution)/shard_map/graph_layers/pallas_call | solution.py:501
  110.1 2.3 %settle.1 = (bf16[256,256]{1,0:T(8,128)(2,1)}, bf16[3072,256]{1,0:T(8,128)(2,1)}) custom-call(bf16[256,256]{1,0:T(8,128)(2,1)} %get-tuple-element.4.node_ref, bf16[3072,256]{1,0:T(8,128)(2,1)} %get-tuple-element.5.edge_ref), custom_call_target="tpu_custom_call" | custom-call | tf_op jit(solution)/shard_map/settle/pallas_call | solution.py:555

commit v7 on v6

--- a/solution.py
+++ b/solution.py
@@ -231,8 +231,6 @@
             def _():
                 list_copy((q + chips - s) % chips).wait_recv()
 
-            available(s)
-
         def from_x(s):
             for f in (2, 3):
                 block = halo_block(s, f)
@@ -255,6 +253,14 @@
             @pl.when((k < chips) & (q + k <= last))
             def _():
                 from_line(q + k, q > 0, DOWN, downs)
+
+            @pl.when((k < chips) & (q >= k))
+            def _():
+                available(q - k)
+
+            @pl.when((k < chips) & (q + k <= last))
+            def _():
+                available(q + k)
 
             for kind, who in ((DOWN, downs), (UP, ups)):
                 for a, least in enumerate(REACH):

time: 113 us -> 112 us (level)
  no operation moved by 1% of the time
where the time goes in v7:
time: 112 us
  Pallas kernels  111 us (99%)
  between operations  1.29 us (1%)
    pallas_call x1, Pallas kernels, shards(): pl.pallas_call(kernel, out_shape=outs, in_specs=[vmem, hbm, smem, smem, s...  109 us
    pallas_call x1, Pallas kernels, shards(): pl.pallas_call(settle_kernel, out_shape=outs, in_specs=[hbm, hbm], out_sp...  2.29 us

profile of v7, /device:TPU:1, one launch (start us, length us, event | category | flops | bytes accessed | tf_op | source)
XLA Modules:
  0.0 112.2 jit_solution(13401169364541378456)
XLA Ops:
  1.3 108.6 %graph_layers.1 = (bf16[256,256]{1,0:T(8,128)(2,1)}, bf16[3072,256]{1,0:T(8,128)(2,1)}) custom-call(bf16[256,256]{1,0:T(8,128)(2,1)} %own_ref.1, bf16[3072,256]{1,0:T(8,128)(2,1)} %edge_ref.1, s32[3072]{0:T(1024)} %send_ref.1, s32[3072]{0:T(1024)} %recv_ref.1, s32[1,1]{1,0:T(1,128)S(6)} %copy.16.live_ref, s32[1,4,128]{2,1,0:T(4,128)} %list_ref.1, ...), custom_call_target="tpu_custom_call" | custom-call | flops 20000000000 | bytes 8388608 | tf_op jit(solution)/shard_map/graph_layers/pallas_call | solution.py:507
  109.9 2.3 %settle.1 = (bf16[256,256]{1,0:T(8,128)(2,1)}, bf16[3072,256]{1,0:T(8,128)(2,1)}) custom-call(bf16[256,256]{1,0:T(8,128)(2,1)} %get-tuple-element.4.node_ref, bf16[3072,256]{1,0:T(8,128)(2,1)} %get-tuple-element.5.edge_ref), custom_call_target="tpu_custom_call" | custom-call | tf_op jit(solution)/shard_map/settle/pallas_call | solution.py:561
